TPU v7x, 256 devices: a whole 4x4x8 slice. The times are simulated.
256 devices in a mesh: au: 8 (over y, core), vert: 16 (over x_lo, z), ch: 2 (over x_hi).
Axes of the slice: x: 4 (x_hi: 2, x_lo: 2; x = x_hi * 2 + x_lo), y: 4, z: 8, core: 2. Of those that a mesh axis runs over, the one named last changes fastest.
Arguments:
- visibilities: bfloat16 [131072, 256], P(('au', 'vert'), 'ch'), may hold values from -6 to 6
- owner_tile: int32 [131072, 1], P(('au', 'vert')), may hold values from 0 to 127; in each aligned block of 1024 rows (0 to 1023, 1024 to 2047, ...) at most 32 rows name the same one
- cell_row: int32 [131072], P(('au', 'vert')), may hold values from 0 to 31
- cell_col: int32 [131072], P(('au', 'vert')), may hold values from 0 to 127
- subcell: int32 [2, 131072], P(None, ('au', 'vert')), may hold values from 0 to 7
- channel_weight: float32 [128], P('ch'), may hold values from 0.2 to 1
Outputs:
- grid: float32 [256, 2048, 256], P('au', 'vert', 'ch')
- continuum: float32 [2, 256, 2048], P('ch', 'au', 'vert')
Inputs may be any that keep to these rules, and one draw needn't show every extreme that they name: `owner_tile`: among the rows of one device (aligned blocks of 1024 rows), no tile is named by more than 32 rows, a bound that some block reaches.
All inputs are finite; a program needn't handle non-finite values.
Results may differ from a plain program's by a relative error of at most 0.0025.
Values may be sent and summed in bfloat16 or wider, within the bound.
A program may use at most 64 MiB of HBM per device.

v0:
```python
import math

import jax
import jax.numpy as jnp
from jax import lax
from jax.sharding import PartitionSpec as P

CHAN = 128
SUPPORT = 8
OVS = 8
TU = 32
TV = 128


SIGMA = 1.5


def shifted(shard, axis, by):
    length = lax.axis_size(axis)
    return lax.ppermute(shard, axis, [(i, (i + by) % length) for i in range(length)])


def taper(distance):
    return jnp.exp(-distance * distance / (2.0 * SIGMA * SIGMA))


def taper_table(local_cell, local_offset, extent):
    cell_index = lax.broadcasted_iota(jnp.int32, (local_cell.shape[0], extent), 1)
    tap_index = cell_index - local_cell[:, None] - 1
    distance = (
        tap_index.astype(jnp.float32)
        - float(SUPPORT // 2 - 1)
        - local_offset[:, None].astype(jnp.float32) / OVS
    )
    return jnp.where((tap_index >= 0) & (tap_index < SUPPORT), taper(distance), 0.0)


def fold_rows(extended, inner_size):
    half_span = SUPPORT // 2
    low_strip = extended[0:half_span]
    high_strip = extended[inner_size + half_span : inner_size + 2 * half_span]
    from_above = shifted(low_strip, "au", -1)
    from_below = shifted(high_strip, "au", 1)
    extended = extended.at[inner_size : inner_size + half_span].add(from_above)
    extended = extended.at[half_span : 2 * half_span].add(from_below)
    return extended[half_span : inner_size + half_span]


def fold_cols(extended, inner_size):
    half_span = SUPPORT // 2
    low_strip = extended[:, 0:half_span]
    high_strip = extended[:, inner_size + half_span : inner_size + 2 * half_span]
    from_right = shifted(low_strip, "vert", -1)
    from_left = shifted(high_strip, "vert", 1)
    extended = extended.at[:, inner_size : inner_size + half_span].add(from_right)
    extended = extended.at[:, half_span : 2 * half_span].add(from_left)
    return extended[:, half_span : inner_size + half_span]


def per_device(visibilities, owner_tile, cell_row, cell_col, subcell, channel_weight):
    count_rows = lax.axis_size("au")
    count_cols = lax.axis_size("vert")
    tile_count = count_rows * count_cols
    row_count = visibilities.shape[0]
    column_count = visibilities.shape[1]
    capacity = row_count * 4 // tile_count
    tile_index = owner_tile[:, 0]
    ranking = jnp.argsort(tile_index, stable=True)
    sorted_tile = tile_index[ranking]
    tile_range = jnp.arange(tile_count, dtype=jnp.int32)
    counts = jnp.sum((tile_index[:, None] == tile_range[None, :]).astype(jnp.int32), axis=0)
    starts = jnp.cumsum(counts) - counts
    sorted_hits = sorted_tile[:, None] == tile_range[None, :]
    row_start = jnp.sum(jnp.where(sorted_hits, starts[None, :], 0), axis=1)
    position = jnp.arange(row_count, dtype=jnp.int32) - row_start
    slot_index = sorted_tile * capacity + position
    packed = ((cell_row * TV + cell_col) * OVS + subcell[0]) * OVS + subcell[1]
    send_values = (
        jnp.zeros((tile_count * capacity, column_count), jnp.bfloat16)
        .at[slot_index]
        .set(visibilities[ranking])
    )
    send_packed = jnp.zeros((tile_count * capacity,), jnp.int32).at[slot_index].set(packed[ranking])
    direct_values = send_values.reshape(tile_count, capacity, column_count)
    direct_packed = send_packed.reshape(tile_count, capacity)
    got_values, got_packed = (
        lax.all_to_all(direct_values, ("au", "vert"), split_axis=0, concat_axis=0, tiled=True),
        lax.all_to_all(direct_packed, ("au", "vert"), split_axis=0, concat_axis=0, tiled=True),
    )
    slot_total = tile_count * capacity
    got_values = got_values.reshape(slot_total, column_count)
    got_packed = got_packed.reshape(slot_total)
    local_row = got_packed // (TV * OVS * OVS)
    local_col = got_packed // (OVS * OVS) % TV
    offset_row = got_packed // OVS % OVS
    offset_col = got_packed % OVS
    extent_row = TU + SUPPORT
    extent_col = TV + SUPPORT
    block_rows = math.gcd(slot_total, 1024)
    block_count = slot_total // block_rows

    def split(array):
        return array.reshape((block_count, block_rows) + array.shape[1:])

    def accumulate(running, pieces):
        values, row_cell, col_cell, row_offset, col_offset = pieces
        weight_row = taper_table(row_cell, row_offset, extent_row)
        weight_col = taper_table(col_cell, col_offset, extent_col)
        kernel = (weight_row[:, :, None] * weight_col[:, None, :]).astype(jnp.bfloat16)
        kernel = kernel.reshape(block_rows, extent_row * extent_col)
        product = lax.dot_general(
            kernel, values, (((0,), (0,)), ((), ())), preferred_element_type=jnp.float32
        )
        return (running + product, None)

    running = jnp.zeros((extent_row * extent_col, column_count), jnp.float32)
    running, ignored = lax.scan(
        accumulate,
        running,
        (
            split(got_values),
            split(local_row),
            split(local_col),
            split(offset_row),
            split(offset_col),
        ),
    )
    extended = running.reshape(extent_row, extent_col, column_count)
    grid_tile = fold_cols(fold_rows(extended, TU), TV)
    paired = grid_tile.reshape(TU, TV, column_count // 2, 2)
    weighted = jnp.sum(paired * channel_weight[None, None, :, None], axis=2)
    partial_sum = jnp.transpose(weighted, (2, 0, 1))
    continuum = lax.psum_scatter(partial_sum, "ch", scatter_dimension=0, tiled=True) / CHAN
    return (grid_tile, continuum)


def solution(mesh):
    in_specs = (
        P(("au", "vert"), "ch"),
        P(("au", "vert"), None),
        P(("au", "vert")),
        P(("au", "vert")),
        P(None, ("au", "vert")),
        P("ch"),
    )
    out_specs = (P("au", "vert", "ch"), P("ch", "au", "vert"))
    return jax.shard_map(
        per_device, mesh=mesh, in_specs=in_specs, out_specs=out_specs, check_vma=False
    )
```

profile of v0, /device:TPU:1, one launch (start us, length us, event | category | flops | bytes accessed | tf_op | source)
XLA Modules:
  0.0 192.1 jit_solution(15198028476306308917)
XLA Ops:
  7.2 1.0 convert_reduce_fusion
  8.2 5.1 %sort.17 = (s32[1024]{0:T(1024)}, s32[1024]{0:T(1024)S(1)}) sort(s32[1024]{0:T(1024)} %bitcast.40, s32[1024]{0:T(1024)S(1)} %iota.34), dimensions={0}, to_apply=%region_0.0 | sort | flops 10240 | bytes 16384 | tf_op jit(solution)/shard_map/jit(argsort)/sort | solution.py:68
  13.2 0.8 fusion.31
  14.0 0.7 fusion.28
  14.7 4.5 %gather_fusion = s32[1024]{0:T(1024)S(1)} fusion(s32[1024]{0:T(1024)S(1)} %bitcast.41, s32[1024]{0:T(1024)S(1)} %get-tuple-element.223), kind=kCustom, calls=%fused_computation | custom fusion | bytes 12288 | tf_op jit(solution)/shard_map/gather | solution.py:69
  19.3 0.1 copy.20
  19.4 0.2 reduce-window.8
  19.5 0.1 reduce.8
  19.7 0.4 select_reduce_fusion
  20.0 4.5 %gather_fusion.1 = s32[1024]{0:T(1024)S(1)} fusion(s32[1024]{0:T(1024)S(1)} %get-tuple-element.224, s32[1024]{0:T(1024)S(1)} %get-tuple-element.223), kind=kCustom, calls=%fused_computation.1 | custom fusion | bytes 12288 | tf_op jit(solution)/shard_map/gather | solution.py:83
  24.6 4.3 %scatter_custom_fusion = s32[4096]{0:T(1024)S(1)} fusion(s32[1024]{0:T(1024)S(1)} %bitcast.57, s32[1024]{0:T(1024)S(1)} %gather_fusion.1, s32[]{:T(128)} %constant.248.clone.1), kind=kCustom, calls=%fused_computation.72 | custom fusion | bytes 16388 | tf_op jit(solution)/shard_map/scatter | solution.py:83
  28.9 0.7 all_to_all.9
  29.6 14.9 %all-to-all-start = ((s32[128,1,32]{2,1,0:T(1,128)}), s32[128,1,32]{2,1,0:T(1,128)S(1)}, u32[]{:S(2)}, u32[]{:S(2)}) async-start(s32[128,1,32]{2,1,0:T(1,128)} %bitcast.7), calls=%async_computation | async-start | bytes 131072 | tf_op jit(solution)/shard_map/all_to_all | solution.py:88
  44.5 7.3 %scatter_custom_fusion.1 = bf16[4096,128]{1,0:T(8,128)(2,1)} fusion(s32[1024]{0:T(1024)S(1)} %bitcast.58, bf16[]{:T(256)} %constant.250.clone.1, bf16[1024,128]{1,0:T(8,128)(2,1)S(1)} %copy-done, s32[1024]{0:T(1024)S(1)} %get-tuple-element.223), kind=kCustom, calls=%fused_computation.31 | custom fusion | bytes 1048578 | tf_op jit(solution)/shard_map/scatter | solution.py:81
  51.9 2.9 %all-to-all-done = s32[128,1,32]{2,1,0:T(1,128)S(1)} async-done(((s32[128,1,32]{2,1,0:T(1,128)}), s32[128,1,32]{2,1,0:T(1,128)S(1)}, u32[]{:S(2)}, u32[]{:S(2)}) %all-to-all-start) | async-done | bytes 16416 | tf_op jit(solution)/shard_map/all_to_all | solution.py:88
  54.8 9.8 %all-to-all-start.1 = ((bf16[128,32,128]{2,1,0:T(8,128)(2,1)}), bf16[128,32,128]{2,1,0:T(8,128)(2,1)}, u32[]{:S(2)}, u32[]{:S(2)}) async-start(bf16[128,32,128]{2,1,0:T(8,128)(2,1)} %bitcast.8), calls=%async_computation.1 | async-start | bytes 2097152 | tf_op jit(solution)/shard_map/all_to_all | solution.py:87
  64.6 0.2 reduce-scatter.2.cloned.1.call-start
  64.8 0.6 broadcast.440
  65.4 0.8 reduce.12
  66.3 0.1 reshape.369
  66.5 26.8 %all-to-all-done.1 = bf16[128,32,128]{2,1,0:T(8,128)(2,1)} async-done(((bf16[128,32,128]{2,1,0:T(8,128)(2,1)}), bf16[128,32,128]{2,1,0:T(8,128)(2,1)}, u32[]{:S(2)}, u32[]{:S(2)}) %all-to-all-start.1) | async-done | bytes 1048608 | tf_op jit(solution)/shard_map/all_to_all | solution.py:87
  93.2 57.9 %while.18 = (s32[]{:T(128)}, f32[5440,128]{1,0:T(8,128)S(1)}, s32[4,1024]{1,0:T(4,128)S(1)}, s32[4,1024]{1,0:T(4,128)S(1)}, s32[4,1024]{1,0:T(4,128)S(1)}, /*ind...) while((s32[]{:T(128)}, f32[5440,128]{1,0:T(8,128)S(1)}, ...), condition=%wide.region_7.8_spmd.clone, body=%wide.region_6.7_spmd.clone.sunk | while | flops 1440763904 | bytes 29606508 | solution.py:117
  93.3 0.3 fusion.39
  93.5 0.1 fusion.40
  93.6 8.0 %multiply_convert_fusion.2 = bf16[1024,40,136]{0,2,1:T(8,128)(2,1)} fusion(f32[1024,136]{0,1:T(8,128)S(1)} %fusion.39, f32[1024,40]{0,1:T(8,128)S(1)} %fusion.40), kind=kLoop, calls=%fused_computation.5.clone.1 | loop fusion | flops 11141120 | bytes 11862016 | tf_op jit(solution)/shard_map/while/body/eval_jaxpr/convert_element_type | solution.py:109
  101.6 6.0 %convolution_add_fusion.2 = f32[5440,128]{1,0:T(8,128)S(1)} fusion(bf16[1024,5440]{0,1:T(8,128)(2,1)} %bitcast.42, f32[5440,128]{1,0:T(8,128)S(1)} %get-tuple-element.286, pred[]{:T(512)S(6)} %compare.42, bf16[4,1024,128]{2,1,0:T(8,128)(2,1)} %get-tuple-element.300, s32[]{:T(128)} %get-tuple-element.285), kind=kOutput, calls=%fused_computation.6.clone.1 | convolution fusion | flops 1427456000 | bytes 16974336 | tf_op jit(solution)/shard_map/while/body/eval_jaxpr/dot_general | solution.py:111
  107.7 0.3 fusion.39
  108.0 0.1 fusion.40
  108.1 8.0 %multiply_convert_fusion.2 = bf16[1024,40,136]{0,2,1:T(8,128)(2,1)} fusion(f32[1024,136]{0,1:T(8,128)S(1)} %fusion.39, f32[1024,40]{0,1:T(8,128)S(1)} %fusion.40), kind=kLoop, calls=%fused_computation.5.clone.1 | loop fusion | flops 11141120 | bytes 11862016 | tf_op jit(solution)/shard_map/while/body/eval_jaxpr/convert_element_type | solution.py:109
  116.1 6.1 %convolution_add_fusion.2 = f32[5440,128]{1,0:T(8,128)S(1)} fusion(bf16[1024,5440]{0,1:T(8,128)(2,1)} %bitcast.42, f32[5440,128]{1,0:T(8,128)S(1)} %get-tuple-element.286, pred[]{:T(512)S(6)} %compare.42, bf16[4,1024,128]{2,1,0:T(8,128)(2,1)} %get-tuple-element.300, s32[]{:T(128)} %get-tuple-element.285), kind=kOutput, calls=%fused_computation.6.clone.1 | convolution fusion | flops 1427456000 | bytes 16974336 | tf_op jit(solution)/shard_map/while/body/eval_jaxpr/dot_general | solution.py:111
  122.2 0.3 fusion.39
  122.5 0.1 fusion.40
  122.6 8.0 %multiply_convert_fusion.2 = bf16[1024,40,136]{0,2,1:T(8,128)(2,1)} fusion(f32[1024,136]{0,1:T(8,128)S(1)} %fusion.39, f32[1024,40]{0,1:T(8,128)S(1)} %fusion.40), kind=kLoop, calls=%fused_computation.5.clone.1 | loop fusion | flops 11141120 | bytes 11862016 | tf_op jit(solution)/shard_map/while/body/eval_jaxpr/convert_element_type | solution.py:109
  130.6 6.1 %convolution_add_fusion.2 = f32[5440,128]{1,0:T(8,128)S(1)} fusion(bf16[1024,5440]{0,1:T(8,128)(2,1)} %bitcast.42, f32[5440,128]{1,0:T(8,128)S(1)} %get-tuple-element.286, pred[]{:T(512)S(6)} %compare.42, bf16[4,1024,128]{2,1,0:T(8,128)(2,1)} %get-tuple-element.300, s32[]{:T(128)} %get-tuple-element.285), kind=kOutput, calls=%fused_computation.6.clone.1 | convolution fusion | flops 1427456000 | bytes 16974336 | tf_op jit(solution)/shard_map/while/body/eval_jaxpr/dot_general | solution.py:111
  136.7 0.3 fusion.39
  137.1 8.0 %multiply_convert_fusion.2 = bf16[1024,40,136]{0,2,1:T(8,128)(2,1)} fusion(f32[1024,136]{0,1:T(8,128)S(1)} %fusion.39, f32[1024,40]{0,1:T(8,128)S(1)} %fusion.40), kind=kLoop, calls=%fused_computation.5.clone.1 | loop fusion | flops 11141120 | bytes 11862016 | tf_op jit(solution)/shard_map/while/body/eval_jaxpr/convert_element_type | solution.py:109
  145.1 6.1 %convolution_add_fusion.2 = f32[5440,128]{1,0:T(8,128)S(1)} fusion(bf16[1024,5440]{0,1:T(8,128)(2,1)} %bitcast.42, f32[5440,128]{1,0:T(8,128)S(1)} %get-tuple-element.286, pred[]{:T(512)S(6)} %compare.42, bf16[4,1024,128]{2,1,0:T(8,128)(2,1)} %get-tuple-element.300, s32[]{:T(128)} %get-tuple-element.285), kind=kOutput, calls=%fused_computation.6.clone.1 | convolution fusion | flops 1427456000 | bytes 16974336 | tf_op jit(solution)/shard_map/while/body/eval_jaxpr/dot_general | solution.py:111
  151.2 2.5 %collective-permute-start = (f32[4,136,128]{2,1,0:T(8,128)S(1)}, f32[4,136,128]{2,1,0:T(8,128)S(1)}, u32[]{:S(2)}, u32[]{:S(2)}) collective-permute-start(f32[4,136,128]{2,1,0:T(8,128)S(1)} %bitcast.51), channel_id=1, source_target_pairs={{0,224},{32,0},{64,32},{96,64},{128,96},{160,128},{192,160},{224,1... | collective-permute-start | bytes 835592 | tf_op jit(solution)/shard_map/ppermute | solution.py:20
  153.7 3.5 %collective-permute-done = f32[4,136,128]{2,1,0:T(8,128)S(1)} collective-permute-done((f32[4,136,128]{2,1,0:T(8,128)S(1)}, f32[4,136,128]{2,1,0:T(8,128)S(1)}, u32[]{:S(2)}, u32[]{:S(2)}) %collective-permute-start) | collective-permute-done | bytes 278560 | tf_op jit(solution)/shard_map/ppermute | solution.py:20
  157.3 2.3 %collective-permute-start.2 = (f32[32,4,128]{2,1,0:T(4,128)S(1)}, f32[32,4,128]{2,1,0:T(4,128)S(1)}, u32[]{:S(2)}, u32[]{:S(2)}) collective-permute-start(f32[32,4,128]{2,1,0:T(4,128)S(1)} %get-tuple-element.213), channel_id=1, source_target_pairs={{0,30},{2,0},{4,2},{6,4},{8,6},{10,8},{12,10},{14,12},{16,14},{18,... | collective-permute-start | bytes 196616 | tf_op jit(solution)/shard_map/ppermute | solution.py:20
  159.6 0.1 slice.151
  159.9 1.1 collective-permute-done.2
  161.0 4.1 %collective-permute-done.3 = f32[32,4,128]{2,1,0:T(4,128)S(1)} collective-permute-done((f32[32,4,128]{2,1,0:T(4,128)S(1)}, f32[32,4,128]{2,1,0:T(4,128)S(1)}, u32[]{:S(2)}, u32[]{:S(2)}) %collective-permute-start.3) | collective-permute-done | bytes 65568 | tf_op jit(solution)/shard_map/ppermute | solution.py:20
  165.1 0.2 slice.156
  165.4 2.1 %copy.22 = f32[32,128,128]{1,0,2:T(8,128)} copy(f32[32,128,128]{2,1,0:T(8,128)S(1)} %slice.156) | data formatting | bytes 4194304 | tf_op jit(solution)/shard_map/slice | solution.py:57
  167.5 2.4 %multiply_reduce_fusion = f32[32,128,2]{1,0,2:T(8,128)} fusion(f32[32,128,64,2]{1,0,3,2:T(8,128)} %bitcast.44, f32[64]{0:T(128)S(1)} %copy-done.3), kind=kLoop, calls=%fused_computation.30 | loop fusion | flops 1040384 | bytes 2130176 | tf_op jit(solution)/shard_map/reduce_sum | solution.py:131
  169.9 14.1 %reduce-scatter.2.cloned.1.call-done = f32[1,32,128]{2,1,0:T(8,128)} async-done(((f32[2,32,128]{2,1,0:T(8,128)}), f32[1,32,128]{2,1,0:T(8,128)}) %reduce-scatter.2.cloned.1.call-update) | async-done | bytes 16400 | tf_op jit(solution)/shard_map/reduce_scatter | solution.py:133
  183.9 1.3 broadcast_multiply_fusion
  (33 shorter events, 0.7 us)
Async XLA Ops:
  7.2 37.4 %copy-start = (bf16[1024,128]{1,0:T(8,128)(2,1)S(1)}, bf16[1024,128]{1,0:T(8,128)(2,1)}, u32[]{:S(2)}) copy-start(bf16[1024,128]{1,0:T(8,128)(2,1)} %param.16) | copy-start | bytes 786436
  7.2 7.5 %copy-start.1 = (s32[1024,1]{0,1:T(1,128)S(1)}, s32[1024,1]{0,1:T(1,128)}, u32[]{:S(2)}) copy-start(s32[1024,1]{0,1:T(1,128)} %param.17) | copy-start | bytes 12292
  29.6 25.2 %all-to-all-start = ((s32[128,1,32]{2,1,0:T(1,128)}), s32[128,1,32]{2,1,0:T(1,128)S(1)}, u32[]{:S(2)}, u32[]{:S(2)}) async-start(s32[128,1,32]{2,1,0:T(1,128)} %bitcast.7), calls=%async_computation | async-start | bytes 131072 | tf_op jit(solution)/shard_map/all_to_all | solution.py:88
  54.8 38.4 %all-to-all-start.1 = ((bf16[128,32,128]{2,1,0:T(8,128)(2,1)}), bf16[128,32,128]{2,1,0:T(8,128)(2,1)}, u32[]{:S(2)}, u32[]{:S(2)}) async-start(bf16[128,32,128]{2,1,0:T(8,128)(2,1)} %bitcast.8), calls=%async_computation.1 | async-start | bytes 2097152 | tf_op jit(solution)/shard_map/all_to_all | solution.py:87
  64.6 119.4 %reduce-scatter.2.cloned.1.call-start = ((), (), s32[]{:S(2)}) async-start(), calls=%async_computation.3 | async-start | bytes 49152 | tf_op jit(solution)/shard_map/reduce_scatter | solution.py:133
  151.2 6.0 %collective-permute-start = (f32[4,136,128]{2,1,0:T(8,128)S(1)}, f32[4,136,128]{2,1,0:T(8,128)S(1)}, u32[]{:S(2)}, u32[]{:S(2)}) collective-permute-start(f32[4,136,128]{2,1,0:T(8,128)S(1)} %bitcast.51), channel_id=1, source_target_pairs={{0,224},{32,0},{64,32},{96,64},{128,96},{160,128},{192,160},{224,1... | collective-permute-start | bytes 835592 | tf_op jit(solution)/shard_map/ppermute | solution.py:20
  153.7 3.6 %collective-permute-start.1 = (f32[4,136,128]{2,1,0:T(8,128)S(1)}, f32[4,136,128]{2,1,0:T(8,128)S(1)}, u32[]{:S(2)}, u32[]{:S(2)}) collective-permute-start(f32[4,136,128]{2,1,0:T(8,128)S(1)} %bitcast.50), channel_id=1, source_target_pairs={{0,32},{32,64},{64,96},{96,128},{128,160},{160,192},{192,224},{224... | collective-permute-start | bytes 835592 | tf_op jit(solution)/shard_map/ppermute | solution.py:20
  157.3 3.6 %collective-permute-start.2 = (f32[32,4,128]{2,1,0:T(4,128)S(1)}, f32[32,4,128]{2,1,0:T(4,128)S(1)}, u32[]{:S(2)}, u32[]{:S(2)}) collective-permute-start(f32[32,4,128]{2,1,0:T(4,128)S(1)} %get-tuple-element.213), channel_id=1, source_target_pairs={{0,30},{2,0},{4,2},{6,4},{8,6},{10,8},{12,10},{14,12},{16,14},{18,... | collective-permute-start | bytes 196616 | tf_op jit(solution)/shard_map/ppermute | solution.py:20
  159.8 5.3 %collective-permute-start.3 = (f32[32,4,128]{2,1,0:T(4,128)S(1)}, f32[32,4,128]{2,1,0:T(4,128)S(1)}, u32[]{:S(2)}, u32[]{:S(2)}) collective-permute-start(f32[32,4,128]{2,1,0:T(4,128)S(1)} %get-tuple-element.212), channel_id=1, source_target_pairs={{0,2},{2,4},{4,6},{6,8},{8,10},{10,12},{12,14},{14,16},{16,18},{18... | collective-permute-start | bytes 196616 | tf_op jit(solution)/shard_map/ppermute | solution.py:20
  165.4 4.5 %copy-start.2 = (f32[32,128,128]{2,1,0:T(8,128)}, f32[32,128,128]{2,1,0:T(8,128)S(1)}, u32[]{:S(2)}) copy-start(f32[32,128,128]{2,1,0:T(8,128)S(1)} %slice.156) | copy-start | bytes 6291460
  165.4 2.1 %copy-start.3 = (f32[64]{0:T(128)S(1)}, f32[64]{0:T(128)}, u32[]{:S(2)}) copy-start(f32[64]{0:T(128)} %param.21) | copy-start | bytes 772
Sparse Core Ops, SparseCore 0:
  170.0 13.8 reduce-scatter.1
where the time goes:
time: 193 us; the launch traced here: 192 us
  waiting for transfers between devices  52.4 us (27%)
  other arithmetic  45.7 us (24%)
  starting transfers between devices  29.7 us (15%)
  local copies, waits for them, and re-layouts  25.6 us (13%)
  matrix products  24.2 us (13%)
  between operations  14.2 us (7%)
    convert_element_type x4, other arithmetic, accumulate(): (weight_row[:, :, None] * weight_col[:, None, :]).astype(jnp.bfloat16)  32 us
    all_to_all x1, waiting for transfers between devices, per_device(): lax.all_to_all(direct_values, ('au', 'vert'), split_axis=0, concat_axis=0...  26.8 us
    dot_general x4, matrix products, accumulate(): lax.dot_general(kernel, values, (((0,), (0,)), ((), ())), preferred_eleme...  24.2 us
    all_to_all x1, starting transfers between devices, per_device(): lax.all_to_all(direct_packed, ('au', 'vert'), split_axis=0, concat_axis=0...  14.9 us
    reduce_scatter x1, waiting for transfers between devices, per_device(): lax.psum_scatter(partial_sum, 'ch', scatter_dimension=0, tiled=True) / CHAN  14.1 us
    all_to_all x1, starting transfers between devices, per_device(): lax.all_to_all(direct_values, ('au', 'vert'), split_axis=0, concat_axis=0...  9.79 us
    ppermute x4, waiting for transfers between devices, shifted(): lax.ppermute(shard, axis, [(i, (i + by) % length) for i in range(length)])  8.69 us
    scatter x1, local copies, waits for them, and re-layouts, per_device(): send_values = jnp.zeros((tile_count * capacity, column_count), jnp.bfloat...  7.34 us
  transfers between devices with their start and end apart: 7, of which 6 were waited for; matrix products, arithmetic and copies ran while one was open for 5% of the time, Pallas kernels for 0%

commit v1 on v0

v1 whole, which is shorter than its diff:
```python
import jax
import jax.numpy as jnp
from jax import lax
from jax.experimental import pallas as pl
from jax.experimental.pallas import tpu as pltpu
from jax.sharding import PartitionSpec as P

MESH = pl.DeviceIdType.MESH
F32 = jnp.float32
BF16 = jnp.bfloat16
I32 = jnp.int32

CHAN = 128
OVS = 8
SIGMA = 1.5
TU = 32
TV = 128
EU = TU + 8
EV = TV + 8
TILES = 128
CAP = 32
ROWS = 1024
COLS = 128
STEPS = 128
GROUP = 8
GROUPS = STEPS // GROUP
DEPTH = GROUP * CAP
UB = 4


def mod(value, by):
    return lax.rem(value + by, by)


def nt(lhs, rhs):
    return lax.dot_general(lhs, rhs, (((1,), (1,)), ((), ())), preferred_element_type=F32)


def nn(lhs, rhs):
    return jnp.dot(lhs, rhs, preferred_element_type=F32)


def flag(mask):
    return jnp.where(mask, 1.0, 0.0)


def kernel(
    vis_ref, tile_ref, pack_ref, weight_ref,
    grid_ref, cont_ref,
    acc, send_v, recv_v, send_m, recv_m, sid_ref, wr_ref, wc_ref,
    row_out, row_in, col_out, col_in, cor_out, cor_in, con_out, con_in,
    send_sem, recv_sem, msend_sem, mrecv_sem, hsend_sem, hrecv_sem, out_sem, line_sem,
):
    au, vert, ch = lax.axis_index("au"), lax.axis_index("vert"), lax.axis_index("ch")
    z, xl = lax.rem(vert, 8), vert // 8
    y, core = au // 2, lax.rem(au, 2)

    def target(group, dz):
        dc, dx, dy = lax.rem(group, 2), lax.rem(group // 2, 2), group // 4
        to_au = mod(y + dy, 4) * 2 + mod(core + dc, 2)
        to_vert = mod(xl + dx, 2) * 8 + mod(z + dz, 8)
        return to_au, to_vert

    barrier = pltpu.get_barrier_semaphore()

    def greet(to_au, to_vert, to_ch, sem):
        pl.semaphore_signal(sem, inc=1, device_id=(to_au, to_vert, to_ch), device_id_type=MESH)

    def greet_line(sem):
        def body(dz, carry):
            to_au, to_vert = target(0, dz)
            greet(to_au, to_vert, ch, sem)
            return carry
        lax.fori_loop(1, 8, body, 0)

    def greet_slab(group, carry):
        to_au, to_vert = target(group, 0)
        greet(to_au, to_vert, ch, barrier)
        return carry

    greet_line(barrier)
    lax.fori_loop(1, GROUPS, greet_slab, 0)
    greet(au, vert, 1 - ch, barrier)

    tile_row = tile_ref[...]
    packed_row = pack_ref[...]
    low = (packed_row & 63).astype(F32)
    middle = ((packed_row >> 6) & 127).astype(F32)
    high = (packed_row >> 13).astype(F32)
    strict = flag(
        lax.broadcasted_iota(I32, (128, 128), 0) < lax.broadcasted_iota(I32, (128, 128), 1)
    ).astype(BF16)
    sub_iota = lax.broadcasted_iota(I32, (128, 128), 0)
    lane_iota = lax.broadcasted_iota(I32, (128, 128), 1)
    ones = jnp.ones((128, 128), BF16)
    before = jnp.zeros((TILES, 128), F32)
    meta_low = jnp.zeros((TILES, 128), F32)
    meta_middle = jnp.zeros((TILES, 128), F32)
    meta_high = jnp.zeros((TILES, 128), F32)
    for part in range(ROWS // 128):
        cut = slice(part * 128, part * 128 + 128)
        hit = flag(sub_iota == tile_row[:, cut])
        hit_low = hit.astype(BF16)
        rank = nn(hit_low, strict) + before
        before = before + nn(hit_low, ones)
        place = jnp.sum(hit * rank, axis=0, keepdims=True).astype(I32)
        sid_ref[:, cut] = tile_row[:, cut] * CAP + place
        lane_hit = flag((sub_iota & (CAP - 1)) == place).astype(BF16)
        meta_low += nt((hit * low[:, cut]).astype(BF16), lane_hit)
        meta_middle += nt((hit * middle[:, cut]).astype(BF16), lane_hit)
        meta_high += nt((hit * high[:, cut]).astype(BF16), lane_hit)
    meta = meta_high * 8192.0 + meta_middle * 64.0 + meta_low
    quarter = lane_iota // CAP
    meta = jnp.where(quarter == lax.rem(sub_iota - z + 8, 4), meta, 0.0)
    send_m[...] = meta.reshape(TILES, 1, 128)
    acc[...] = jnp.zeros_like(acc)

    pl.semaphore_wait(barrier, 23)
    greet_line(line_sem)
    pl.semaphore_wait(line_sem, 7)

    def copies(group, dz):
        to_au, to_vert = target(group, dz)
        tile = to_au * 16 + to_vert
        step = group * GROUP + dz
        device = (to_au, to_vert, ch)
        return (
            pltpu.make_async_remote_copy(
                src_ref=send_v.at[tile], dst_ref=recv_v.at[step],
                send_sem=send_sem.at[step], recv_sem=recv_sem.at[step],
                device_id=device, device_id_type=MESH,
            ),
            pltpu.make_async_remote_copy(
                src_ref=send_m.at[tile], dst_ref=recv_m.at[step],
                send_sem=msend_sem.at[step], recv_sem=mrecv_sem.at[step],
                device_id=device, device_id_type=MESH,
            ),
        )

    def fill(group, first):
        to_au, to_vert = target(group, 0)
        base = to_au * 16 + (to_vert // 8) * 8
        slot = lax.broadcasted_iota(I32, (DEPTH, ROWS), 0) + base * CAP
        pick = flag(slot == sid_ref[...]).astype(BF16)
        send_v[pl.ds(base, GROUP)] = nn(pick, vis_ref[...]).astype(BF16).reshape(GROUP, CAP, COLS)

        def start(dz, carry):
            for copy in copies(group, dz):
                copy.start()
            return carry
        lax.fori_loop(first, GROUP, start, 0)

    fill(0, 1)
    mine = au * 16 + vert
    recv_v[0] = send_v[mine]
    recv_m[0] = send_m[mine]

    def fill_step(group, carry):
        fill(group, 0)
        return carry
    lax.fori_loop(1, GROUPS, fill_step, 0)

    def weights(meta_line):
        m = meta_line.astype(I32)
        a, b, o, p = m >> 13, (m >> 6) & 127, (m >> 3) & 7, m & 7

        def taper(index, extent, inner, cell, offset):
            cell_at = jnp.where(index < inner + 4, index, index - extent) - cell
            x = cell_at.astype(F32) - offset.astype(F32) / OVS
            tap = cell_at + 3
            return jnp.where((tap >= 0) & (tap < 8), jnp.exp(-x * x / (2.0 * SIGMA * SIGMA)), 0.0)

        wr_ref[...] = taper(lax.broadcasted_iota(I32, (EU, DEPTH), 0), EU, TU, a, o)
        wc_ref[...] = taper(lax.broadcasted_iota(I32, (EV, DEPTH), 0), EV, TV, b, p)

    def add_chunk(group):
        base = group * GROUP
        line = jnp.concatenate(
            [
                jnp.sum(recv_m[pl.ds(base, 4)].reshape(4, 128), axis=0, keepdims=True),
                jnp.sum(recv_m[pl.ds(base + 4, 4)].reshape(4, 128), axis=0, keepdims=True),
            ],
            axis=1,
        )
        weights(line)
        values = recv_v[pl.ds(base, GROUP)].reshape(DEPTH, COLS)

        def some(block, carry):
            u = block * UB
            col = wc_ref[...]
            taps = jnp.concatenate([col * wr_ref[pl.ds(u + i, 1), :] for i in range(UB)], axis=0)
            product = nn(taps.astype(BF16), values).reshape(UB, EV, COLS)
            acc[pl.ds(u, UB)] += product
            return carry
        lax.fori_loop(0, EU // UB, some, 0)

    def arrive(group, first):
        def body(dz, carry):
            for copy in copies(group, dz):
                copy.wait_recv()
            return carry
        lax.fori_loop(first, GROUP, body, 0)

    arrive(0, 1)
    add_chunk(0)

    def chunk_step(group, carry):
        arrive(group, 0)
        add_chunk(group)
        return carry
    lax.fori_loop(1, GROUPS, chunk_step, 0)

    row_out[...] = acc[TU:EU, 0:TV].reshape(2, 4 * TV, COLS).astype(BF16)
    col_out[...] = acc[0:TU, TV:EV].reshape(TU * 8, COLS).astype(BF16)
    cor_out[...] = acc[TU:EU, TV:EV].reshape(64, COLS).astype(BF16)
    down, up = mod(au + 1, 8), mod(au + 7, 8)
    right, left = mod(vert + 1, 16), mod(vert + 15, 16)

    def halo(src, dst, number, to_au, to_vert):
        return pltpu.make_async_remote_copy(
            src_ref=src, dst_ref=dst, send_sem=hsend_sem.at[number], recv_sem=hrecv_sem.at[number],
            device_id=(to_au, to_vert, ch), device_id_type=MESH,
        )

    halos = [
        halo(row_out.at[0], row_in.at[0], 0, down, vert),
        halo(row_out.at[1], row_in.at[1], 1, up, vert),
        halo(col_out, col_in.at[0], 2, au, right),
        halo(col_out, col_in.at[1], 3, au, left),
        halo(cor_out, cor_in.at[0], 4, down, right),
        halo(cor_out, cor_in.at[1], 5, down, left),
        halo(cor_out, cor_in.at[2], 6, up, right),
        halo(cor_out, cor_in.at[3], 7, up, left),
    ]
    for copy in halos:
        copy.start()

    def drain(group, first):
        def body(dz, carry):
            for copy in copies(group, dz):
                copy.wait_send()
            return carry
        lax.fori_loop(first, GROUP, body, 0)

    drain(0, 1)

    def drain_step(group, carry):
        drain(group, 0)
        return carry
    lax.fori_loop(1, GROUPS, drain_step, 0)

    for copy in halos:
        copy.wait()

    front = lax.broadcasted_iota(I32, (1, 8, COLS), 1) < 4
    acc[0:4, 0:TV] += row_in[0].astype(F32).reshape(4, TV, COLS)
    acc[TU - 4 : TU, 0:TV] += row_in[1].astype(F32).reshape(4, TV, COLS)
    from_left = col_in[0].astype(F32).reshape(TU, 8, COLS)
    from_right = col_in[1].astype(F32).reshape(TU, 8, COLS)
    acc[0:TU, 0:8] += jnp.where(front, from_left, 0.0)
    acc[0:TU, TV - 8 : TV] += jnp.where(front, 0.0, from_right)
    corners = [cor_in[i].astype(F32).reshape(8, 8, COLS) for i in range(4)]
    acc[0:4, 0:8] += jnp.where(front, corners[0][0:4], 0.0)
    acc[0:4, TV - 8 : TV] += jnp.where(front, 0.0, corners[1][0:4])
    acc[TU - 4 : TU, 0:8] += jnp.where(front, corners[2][4:8], 0.0)
    acc[TU - 4 : TU, TV - 8 : TV] += jnp.where(front, 0.0, corners[3][4:8])

    out = pltpu.make_async_copy(acc.at[pl.ds(0, TU), pl.ds(0, TV)], grid_ref, out_sem)
    out.start()

    weight = weight_ref[...]
    weight_high = weight.astype(BF16).astype(F32)
    weight_low = weight - weight_high
    kind = jnp.where(sub_iota < 64, weight_high, weight_low)
    result_at = (lane_iota & 1) * TU

    def channel_sum(u, total):
        cells = acc[pl.ds(u, 1), 0:TV].reshape(TV, COLS)
        cells_high = cells.astype(BF16)
        cells_low = (cells - cells_high.astype(F32)).astype(BF16)
        pick = jnp.where((sub_iota & 63) == result_at + u, kind, 0.0).astype(BF16)
        return total + nt(pick, cells_high) + nt(pick, cells_low)

    total = lax.fori_loop(0, TU, channel_sum, jnp.zeros((128, TV), F32))
    con_out[...] = total[0:64] + total[64:128]
    swap = pltpu.make_async_remote_copy(
        src_ref=con_out.at[pl.ds(pl.multiple_of((1 - ch) * TU, TU), TU)], dst_ref=con_in,
        send_sem=hsend_sem.at[8], recv_sem=hrecv_sem.at[8],
        device_id=(au, vert, 1 - ch), device_id_type=MESH,
    )
    swap.start()
    swap.wait()
    own = con_out[pl.ds(pl.multiple_of(ch * TU, TU), TU)]
    cont_ref[...] = (own + con_in[...]) * (1.0 / CHAN)
    out.wait()


def per_device(visibilities, owner_tile, cell_row, cell_col, subcell, channel_weight):
    tile = owner_tile.reshape(1, ROWS)
    packed = ((cell_row * TV + cell_col) * OVS + subcell[0]) * OVS + subcell[1]
    weight = jnp.repeat(channel_weight, 2).reshape(1, COLS)
    vmem = pl.BlockSpec(memory_space=pltpu.VMEM)
    grid, cont = pl.pallas_call(
        kernel,
        out_shape=(
            jax.ShapeDtypeStruct((TU, TV, COLS), F32),
            jax.ShapeDtypeStruct((TU, TV), F32),
        ),
        in_specs=[vmem] * 4,
        out_specs=(pl.BlockSpec(memory_space=pl.ANY), vmem),
        scratch_shapes=[
            pltpu.VMEM((EU, EV, COLS), F32),
            pltpu.VMEM((TILES, CAP, COLS), BF16),
            pltpu.VMEM((STEPS, CAP, COLS), BF16),
            pltpu.VMEM((TILES, 1, 128), F32),
            pltpu.VMEM((STEPS, 1, 128), F32),
            pltpu.VMEM((1, ROWS), I32),
            pltpu.VMEM((EU, DEPTH), F32),
            pltpu.VMEM((EV, DEPTH), F32),
            pltpu.VMEM((2, 4 * TV, COLS), BF16),
            pltpu.VMEM((2, 4 * TV, COLS), BF16),
            pltpu.VMEM((TU * 8, COLS), BF16),
            pltpu.VMEM((2, TU * 8, COLS), BF16),
            pltpu.VMEM((64, COLS), BF16),
            pltpu.VMEM((4, 64, COLS), BF16),
            pltpu.VMEM((2 * TU, TV), F32),
            pltpu.VMEM((TU, TV), F32),
            pltpu.SemaphoreType.DMA((STEPS,)),
            pltpu.SemaphoreType.DMA((STEPS,)),
            pltpu.SemaphoreType.DMA((STEPS,)),
            pltpu.SemaphoreType.DMA((STEPS,)),
            pltpu.SemaphoreType.DMA((9,)),
            pltpu.SemaphoreType.DMA((9,)),
            pltpu.SemaphoreType.DMA,
            pltpu.SemaphoreType.REGULAR,
        ],
        compiler_params=pltpu.CompilerParams(
            collective_id=0, has_side_effects=True, vmem_limit_bytes=40 * 2**20
        ),
        name="gridding",
    )(visibilities, tile, packed.reshape(1, ROWS), weight)
    return grid, cont.reshape(1, TU, TV)


def solution(mesh):
    in_specs = (
        P(("au", "vert"), "ch"),
        P(("au", "vert"), None),
        P(("au", "vert")),
        P(("au", "vert")),
        P(None, ("au", "vert")),
        P("ch"),
    )
    out_specs = (P("au", "vert", "ch"), P("ch", "au", "vert"))
    return jax.shard_map(
        per_device, mesh=mesh, in_specs=in_specs, out_specs=out_specs, check_vma=False
    )
```

time: 193 us -> 87.3 us (0.45)
  Pallas kernels: 0 us -> 80.4 us
  waiting for transfers between devices: 52.4 us -> 0 us
  other arithmetic: 45.7 us -> 0.71 us
  starting transfers between devices: 29.7 us -> 0 us
  matrix products: 24.2 us -> 0 us
  local copies, waits for them, and re-layouts: 25.6 us -> 5.21 us
  between operations: 14.2 us -> 0.65 us
    pallas_call x0 -> x1, Pallas kernels: none -> 80.4 us  [per_device(): pl.pallas_call(kernel, out_shape=(jax.ShapeDtypeStruct((TU, TV, COLS), F3...]
    convert_element_type x4 -> x0, other arithmetic: 32 us -> none  [accumulate(): (weight_row[:, :, None] * weight_col[:, None, :]).astype(jnp.bfloat16)]
    all_to_all x2 -> x0, waiting for transfers between devices: 29.7 us -> none  [the longest x1 26.8 us: per_device(): lax.all_to_all(direct_values, ('au', 'vert'), split_axis=0, concat_axis=0...]
    all_to_all x2 -> x0, starting transfers between devices: 24.7 us -> none  [the longest x1 14.9 us: per_device(): lax.all_to_all(direct_packed, ('au', 'vert'), split_axis=0, concat_axis=0...]
    dot_general x4 -> x0, matrix products: 24.2 us -> none  [accumulate(): lax.dot_general(kernel, values, (((0,), (0,)), ((), ())), preferred_eleme...]
    reduce_scatter x1 -> x0, waiting for transfers between devices: 14.1 us -> none  [per_device(): lax.psum_scatter(partial_sum, 'ch', scatter_dimension=0, tiled=True) / CHAN]
    scatter x2 -> x0, local copies, waits for them, and re-layouts: 11.7 us -> none  [the longest x1 7.34 us: per_device(): send_values = jnp.zeros((tile_count * capacity, column_count), jnp.bfloat...]
    gather x2 -> x0, local copies, waits for them, and re-layouts: 9.06 us -> none  [the longest x1 4.53 us: per_device(): sorted_tile = tile_index[ranking]]
  transfers between devices with their start and end apart: 7 -> 0, of which waited for: 6 -> 0; matrix products, arithmetic and copies ran while one was open for 5% -> 0% of each run, Pallas kernels for 0% -> 0%
where the time goes in v1:
time: 87.3 us; the launch traced here: 87 us
  Pallas kernels  80.4 us (92%)
  local copies, waits for them, and re-layouts  5.21 us (6%)
    pallas_call x1, Pallas kernels, per_device(): pl.pallas_call(kernel, out_shape=(jax.ShapeDtypeStruct((TU, TV, COLS), F3...  80.4 us
    unnamed x6, local copies, waits for them, and re-layouts  3.56 us

profile of v1, /device:TPU:1, one launch (start us, length us, event | category | flops | bytes accessed | tf_op | source)
XLA Modules:
  0.0 87.0 jit_solution(12099859601068607880)
XLA Ops:
  0.6 0.8 fusion
  1.4 0.7 multiply_add_fusion
  2.1 0.7 broadcast_in_dim.3
  2.9 0.1 reshape_reshape.3.weight_ref
  3.0 0.0 copy-start
  3.0 0.9 %copy-done = bf16[1024,128]{1,0:T(8,128)(2,1)S(1)} copy-done((bf16[1024,128]{1,0:T(8,128)(2,1)S(1)}, bf16[1024,128]{1,0:T(8,128)(2,1)}, u32[]{:S(2)}) %copy-start) | copy-done | bytes 262168
  4.0 0.0 copy-start.1
  4.0 0.7 copy-done.1
  4.6 80.4 %gridding.1 = (f32[32,128,128]{2,1,0:T(8,128)S(1)}, f32[32,128]{1,0:T(8,128)S(1)}) custom-call(bf16[1024,128]{1,0:T(8,128)(2,1)S(1)} %copy-done, s32[1,1024]{1,0:T(1,128)S(1)} %bitcast.7, s32[1,1024]{1,0:T(1,128)S(1)} %bitcast.5, f32[1,128]{1,0:T(1,128)S(1)} %reshape_reshape.3.weight_ref), custom_call_target="tpu_custom_call" | custom-call | tf_op jit(solution)/shard_map/gridding/pallas_call | solution.py:303
  85.1 1.3 %copy.10 = f32[32,128,128]{2,1,0:T(8,128)} copy(f32[32,128,128]{2,1,0:T(8,128)S(1)} %get-tuple-element.10) | data formatting | bytes 4194304
  86.4 0.6 copy.11
Async XLA Ops:
  3.0 1.0 %copy-start = (bf16[1024,128]{1,0:T(8,128)(2,1)S(1)}, bf16[1024,128]{1,0:T(8,128)(2,1)}, u32[]{:S(2)}) copy-start(bf16[1024,128]{1,0:T(8,128)(2,1)} %vis_ref.1) | copy-start | bytes 786436
  4.0 0.7 copy-start.1

commit v2 on v1

v2 whole, which is shorter than its diff:
```python
import jax
import jax.numpy as jnp
from jax import lax
from jax.experimental import pallas as pl
from jax.experimental.pallas import tpu as pltpu
from jax.sharding import PartitionSpec as P

MESH = pl.DeviceIdType.MESH
F32 = jnp.float32
BF16 = jnp.bfloat16
I32 = jnp.int32

CHAN = 128
OVS = 8
SIGMA = 1.5
TU = 32
TV = 128
EU = TU + 8
EV = TV + 8
TILES = 128
CAP = 32
ROWS = 1024
COLS = 128
STEPS = 128
GROUP = 8
GROUPS = STEPS // GROUP
DEPTH = GROUP * CAP
UB = 4
EARLY = 4


def mod(value, by):
    return lax.rem(value + by, by)


def nt(lhs, rhs):
    return lax.dot_general(lhs, rhs, (((1,), (1,)), ((), ())), preferred_element_type=F32)


def nn(lhs, rhs):
    return jnp.dot(lhs, rhs, preferred_element_type=F32)


def flag(mask):
    return jnp.where(mask, 1.0, 0.0)


def kernel(
    vis_hbm, tile_hbm, row_hbm, col_hbm, sub_hbm, weight_hbm,
    grid_hbm, cont_hbm,
    vis_ref, tile_ref, cell_row_ref, cell_col_ref, sub_ref, weight_ref, grid_ref, cont_ref,
    col_acc, row_acc, send_v, recv_v, send_m, recv_m, sid_ref, wr_ref, wc_ref,
    row_out, row_in, col_out, col_in, cor_out, cor_in,
    sum_main, sum_edge, sum_mid_in, sum_row_in, sum_col_in, sum_cor_in,
    load_sem, store_sem, send_sem, recv_sem, hsend_sem, hrecv_sem, ssend_sem, srecv_sem, line_sem, twin_sem,
):
    au, vert, ch = lax.axis_index("au"), lax.axis_index("vert"), lax.axis_index("ch")
    z, xl = lax.rem(vert, 8), vert // 8
    y, core = au // 2, lax.rem(au, 2)

    def target(group, dz):
        dc, dx, dy = lax.rem(group, 2), lax.rem(group // 2, 2), group // 4
        to_au = mod(y + dy, 4) * 2 + mod(core + dc, 2)
        to_vert = mod(xl + dx, 2) * 8 + mod(z + dz, 8)
        return to_au, to_vert

    loads = [
        pltpu.make_async_copy(src, dst, load_sem.at[i])
        for i, (src, dst) in enumerate([
            (tile_hbm, tile_ref), (row_hbm, cell_row_ref), (col_hbm, cell_col_ref),
            (sub_hbm, sub_ref), (weight_hbm, weight_ref), (vis_hbm, vis_ref),
        ])
    ]
    for load in loads:
        load.start()
    barrier = pltpu.get_barrier_semaphore()

    def greet(to_au, to_vert, to_ch, sem):
        pl.semaphore_signal(sem, inc=1, device_id=(to_au, to_vert, to_ch), device_id_type=MESH)

    def greet_line(sem):
        for dz in range(1, 8):
            greet(*target(0, dz), ch, sem)

    greet_line(barrier)
    for group in range(1, GROUPS):
        greet(*target(group, 0), ch, barrier)
    greet(au, vert, 1 - ch, barrier)
    grid_ref[...] = jnp.zeros_like(grid_ref)
    col_acc[...] = jnp.zeros_like(col_acc)
    row_acc[...] = jnp.zeros_like(row_acc)
    sum_edge[...] = jnp.zeros_like(sum_edge)
    for load in loads:
        load.wait()

    tile_row = tile_ref[...]
    low = (sub_ref[0:1, :] * OVS + sub_ref[1:2, :]).astype(F32)
    middle = cell_col_ref[...].astype(F32)
    high = cell_row_ref[...].astype(F32)
    strict = flag(
        lax.broadcasted_iota(I32, (128, 128), 0) < lax.broadcasted_iota(I32, (128, 128), 1)
    ).astype(BF16)
    sub_iota = lax.broadcasted_iota(I32, (128, 128), 0)
    lane_iota = lax.broadcasted_iota(I32, (128, 128), 1)
    ones = jnp.ones((128, 128), BF16)
    before = jnp.zeros((TILES, 128), F32)
    meta_low = jnp.zeros((TILES, 128), F32)
    meta_middle = jnp.zeros((TILES, 128), F32)
    meta_high = jnp.zeros((TILES, 128), F32)
    for part in range(ROWS // 128):
        cut = slice(part * 128, part * 128 + 128)
        hit = flag(sub_iota == tile_row[:, cut])
        hit_low = hit.astype(BF16)
        rank = nn(hit_low, strict) + before
        before = before + nn(hit_low, ones)
        place = jnp.sum(hit * rank, axis=0, keepdims=True).astype(I32)
        sid_ref[:, cut] = tile_row[:, cut] * CAP + place
        lane_hit = flag((sub_iota & (CAP - 1)) == place).astype(BF16)
        meta_low += nt((hit * low[:, cut]).astype(BF16), lane_hit)
        meta_middle += nt((hit * middle[:, cut]).astype(BF16), lane_hit)
        meta_high += nt((hit * high[:, cut]).astype(BF16), lane_hit)
    meta = meta_high * 8192.0 + meta_middle * 64.0 + meta_low
    quarter = lane_iota // CAP
    meta = jnp.where(quarter == lax.rem(sub_iota - z + 8, 4), meta, 0.0)
    send_m[...] = meta.reshape(TILES, 1, 128)

    def copies(group, dz):
        to_au, to_vert = target(group, dz)
        tile = to_au * 16 + to_vert
        step = group * GROUP + dz
        device = (to_au, to_vert, ch)
        return [
            pltpu.make_async_remote_copy(
                src_ref=src.at[tile], dst_ref=dst.at[step],
                send_sem=send_sem.at[kind], recv_sem=recv_sem.at[kind, group],
                device_id=device, device_id_type=MESH,
            )
            for kind, (src, dst) in enumerate([(send_v, recv_v), (send_m, recv_m)])
        ]

    def fill(group):
        to_au, to_vert = target(group, 0)
        base = to_au * 16 + (to_vert // 8) * 8
        slot = lax.broadcasted_iota(I32, (DEPTH, ROWS), 0) + base * CAP
        pick = flag(slot == sid_ref[...]).astype(BF16)
        send_v[pl.ds(base, GROUP)] = nn(pick, vis_ref[...]).astype(BF16).reshape(GROUP, CAP, COLS)

    def start(group, first):
        for dz in range(first, GROUP):
            for copy in copies(group, dz):
                copy.start()

    pl.semaphore_wait(barrier, 23)
    greet_line(line_sem)
    fill(0)
    start(0, 1)
    mine = au * 16 + vert
    recv_v[0] = send_v[mine]
    recv_m[0] = send_m[mine]
    for group in range(1, EARLY):
        fill(group)
    pl.semaphore_wait(line_sem, 7)
    greet(au, vert, 1 - ch, twin_sem)
    for group in range(1, EARLY):
        start(group, 0)

    def fill_step(group, carry):
        fill(group)
        start(group, 0)
        return carry
    lax.fori_loop(EARLY, GROUPS, fill_step, 0)

    def weights(meta_line):
        m = meta_line.astype(I32)
        a, b, o, p = m >> 13, (m >> 6) & 127, (m >> 3) & 7, m & 7

        def taper(index, extent, inner, cell, offset):
            cell_at = jnp.where(index < inner + 4, index, index - extent) - cell
            x = cell_at.astype(F32) - offset.astype(F32) / OVS
            tap = cell_at + 3
            return jnp.where((tap >= 0) & (tap < 8), jnp.exp(-x * x / (2.0 * SIGMA * SIGMA)), 0.0)

        depth = m.shape[1]
        wr_ref[:, 0:depth] = taper(lax.broadcasted_iota(I32, (EU, depth), 0), EU, TU, a, o)
        wc_ref[:, 0:depth] = taper(lax.broadcasted_iota(I32, (EV, depth), 0), EV, TV, b, p)

    def arrived(group, first, count):
        span = pl.ds(group * GROUP + first, count)
        for kind, ref in enumerate([recv_v, recv_m]):
            pltpu.make_async_copy(ref.at[span], ref.at[span], recv_sem.at[kind, group]).wait()

    def add_chunk(group, groups, after_rows):
        base = group * GROUP
        depth = groups * DEPTH
        line = jnp.concatenate(
            [
                jnp.sum(recv_m[pl.ds(base + 4 * i, 4)].reshape(4, 128), axis=0, keepdims=True)
                for i in range(2 * groups)
            ],
            axis=1,
        )
        weights(line)
        values = recv_v[pl.ds(base, groups * GROUP)].reshape(depth, COLS)
        for u in [*range(TU, EU, UB), *range(0, TU, UB)]:
            if u == 0:
                after_rows()
            col = wc_ref[:, 0:depth]
            taps = jnp.concatenate([col * wr_ref[u + i : u + i + 1, 0:depth] for i in range(UB)], axis=0)
            product = nn(taps.astype(BF16), values).reshape(UB, EV, COLS)
            if u < TU:
                grid_ref[u : u + UB] += product[:, 0:TV]
                col_acc[u : u + UB] += product[:, TV:EV]
            else:
                row_acc[u - TU : u - TU + UB] += product

    arrived(0, 1, GROUP - 1)
    add_chunk(0, 1, lambda: None)

    def chunk_step(pair, carry):
        group = 2 * pair + 1
        arrived(group, 0, GROUP)
        arrived(group + 1, 0, GROUP)
        add_chunk(group, 2, lambda: None)
        return carry
    lax.fori_loop(0, GROUPS // 2 - 1, chunk_step, 0)
    down, up = mod(au + 1, 8), mod(au + 7, 8)
    right, left = mod(vert + 1, 16), mod(vert + 15, 16)

    def halo(src, dst, number, to_au, to_vert):
        return pltpu.make_async_remote_copy(
            src_ref=src, dst_ref=dst, send_sem=hsend_sem.at[number], recv_sem=hrecv_sem.at[number],
            device_id=(to_au, to_vert, ch), device_id_type=MESH,
        )

    row_halos = [
        halo(row_out.at[0], row_in.at[0], 0, down, vert),
        halo(row_out.at[1], row_in.at[1], 1, up, vert),
        halo(cor_out, cor_in.at[0], 2, down, right),
        halo(cor_out, cor_in.at[1], 3, down, left),
        halo(cor_out, cor_in.at[2], 4, up, right),
        halo(cor_out, cor_in.at[3], 5, up, left),
    ]
    col_halos = [
        halo(col_out, col_in.at[0], 6, au, right),
        halo(col_out, col_in.at[1], 7, au, left),
    ]

    def send_rows():
        row_out[...] = row_acc[:, 0:TV].reshape(2, 4 * TV, COLS).astype(BF16)
        cor_out[...] = row_acc[:, TV:EV].reshape(64, COLS).astype(BF16)
        for copy in row_halos:
            copy.start()

    arrived(GROUPS - 1, 0, GROUP)
    add_chunk(GROUPS - 1, 1, send_rows)
    col_out[...] = col_acc[...].reshape(TU * 8, COLS).astype(BF16)
    for copy in col_halos:
        copy.start()

    spread = flag(
        lax.broadcasted_iota(I32, (COLS // 2, COLS), 0) == lax.broadcasted_iota(I32, (COLS // 2, COLS), 1) // 2
    ).astype(BF16)
    weight = jnp.zeros((1, COLS), F32)
    rest = weight_ref[...]
    for part in range(3):
        piece = rest.astype(BF16)
        rest = rest - piece.astype(F32)
        weight += nn(piece, spread)
    weight_high = weight.astype(BF16).astype(F32)
    line = lax.broadcasted_iota(I32, (16, COLS), 0)
    mine_only = (line & 1) == (lax.broadcasted_iota(I32, (16, COLS), 1) & 1)
    pick = jnp.where(line < 2, weight_high, jnp.where(line < 4, weight - weight_high, 0.0))
    pick = jnp.where(mine_only, pick, 0.0).astype(BF16)
    pick = jnp.concatenate([pick, pick], axis=1)

    def channel_sum(u):
        if u < TU:
            cells = jnp.concatenate([grid_ref[u], col_acc[u]], axis=0)
        else:
            cells = row_acc[u - TU]
        cells_high = cells.astype(BF16)
        cells_low = (cells - cells_high.astype(F32)).astype(BF16)
        result = nt(pick, jnp.concatenate([cells_high, cells_low], axis=1))
        return result[0:2] + result[2:4]

    for u in range(0, EU, 8):
        sums = [channel_sum(u + i) for i in range(8)]
        for q in range(2):
            whole = jnp.concatenate([one[q : q + 1] for one in sums], axis=0)
            sum_main[q, u : u + 8, :] = whole[:, 0:TV]
            sum_edge[q, u : u + 8, 0:8] = whole[:, TV:EV]

    def part(src, dst, number, to_au, to_vert, to_ch):
        return pltpu.make_async_remote_copy(
            src_ref=src, dst_ref=dst, send_sem=ssend_sem.at[number], recv_sem=srecv_sem.at[number],
            device_id=(to_au, to_vert, to_ch), device_id_type=MESH,
        )

    parts = [part(sum_main.at[1 - ch, pl.ds(0, TU)], sum_mid_in, 0, au, vert, 1 - ch)]
    for other in range(2):
        q = 1 - ch if other else ch
        rows, cols, edge = pl.ds(TU, 8), pl.ds(0, TU), 1 + 8 * other
        parts += [
            part(sum_main.at[q, rows], sum_row_in.at[other, 0], edge, down, vert, q),
            part(sum_main.at[q, rows], sum_row_in.at[other, 1], edge + 1, up, vert, q),
            part(sum_edge.at[q, cols], sum_col_in.at[other, 0], edge + 2, au, right, q),
            part(sum_edge.at[q, cols], sum_col_in.at[other, 1], edge + 3, au, left, q),
            part(sum_edge.at[q, rows], sum_cor_in.at[other, 0], edge + 4, down, right, q),
            part(sum_edge.at[q, rows], sum_cor_in.at[other, 1], edge + 5, down, left, q),
            part(sum_edge.at[q, rows], sum_cor_in.at[other, 2], edge + 6, up, right, q),
            part(sum_edge.at[q, rows], sum_cor_in.at[other, 3], edge + 7, up, left, q),
        ]
    pl.semaphore_wait(twin_sem, 1)
    for copy in parts:
        copy.start()

    for kind, ref in enumerate([recv_v, recv_m]):
        span = pl.ds(1, STEPS - 1)
        pltpu.make_async_copy(ref.at[span], ref.at[span], send_sem.at[kind]).wait()
    for copy in row_halos + col_halos:
        copy.wait()

    front = lax.broadcasted_iota(I32, (1, 8, COLS), 1) < 4
    grid_ref[0:4, 0:TV] += row_in[0].astype(F32).reshape(4, TV, COLS)
    grid_ref[TU - 4 : TU, 0:TV] += row_in[1].astype(F32).reshape(4, TV, COLS)
    from_left = col_in[0].astype(F32).reshape(TU, 8, COLS)
    from_right = col_in[1].astype(F32).reshape(TU, 8, COLS)
    grid_ref[0:TU, 0:8] += jnp.where(front, from_left, 0.0)
    grid_ref[0:TU, TV - 8 : TV] += jnp.where(front, 0.0, from_right)
    corners = [cor_in[i].astype(F32).reshape(8, 8, COLS) for i in range(4)]
    grid_ref[0:4, 0:8] += jnp.where(front, corners[0][0:4], 0.0)
    grid_ref[0:4, TV - 8 : TV] += jnp.where(front, 0.0, corners[1][0:4])
    grid_ref[TU - 4 : TU, 0:8] += jnp.where(front, corners[2][4:8], 0.0)
    grid_ref[TU - 4 : TU, TV - 8 : TV] += jnp.where(front, 0.0, corners[3][4:8])

    stores = [
        pltpu.make_async_copy(grid_ref.at[pl.ds(u, 8)], grid_hbm.at[pl.ds(u, 8)], store_sem.at[u // 8])
        for u in range(0, TU, 8)
    ]
    for store in stores:
        store.start()
    for copy in parts:
        copy.wait()
    top = lax.broadcasted_iota(I32, (8, TV), 0) < 4
    lane = lax.broadcasted_iota(I32, (TU, TV), 1)

    def sides(from_left, from_right, rows):
        at = lane[0:rows]
        return jnp.where(at < 4, from_left, 0.0) + jnp.where(at >= TV - 4, pltpu.roll(from_right, TV - 8, 1), 0.0)

    total = sum_main[ch, 0:TU] + sum_mid_in[...]
    first = jnp.zeros((8, TV), F32)
    last = jnp.zeros((8, TV), F32)
    for other in range(2):
        total += sides(sum_col_in[other, 0], sum_col_in[other, 1], TU)
        first += sum_row_in[other, 0] + sides(sum_cor_in[other, 0], sum_cor_in[other, 1], 8)
        last += sum_row_in[other, 1] + sides(sum_cor_in[other, 2], sum_cor_in[other, 3], 8)
    cont_ref[...] = total * (1.0 / CHAN)
    cont_ref[0:8] += jnp.where(top, first, 0.0) * (1.0 / CHAN)
    cont_ref[TU - 8 : TU] += jnp.where(top, 0.0, last) * (1.0 / CHAN)
    store = pltpu.make_async_copy(cont_ref, cont_hbm, store_sem.at[4])
    store.start()
    for store in [*stores, store]:
        store.wait()


def handover(grid_in, cont_in, grid_out, cont_out, grid_ref, cont_ref, in_sem, out_sem):
    cuts = [pl.ds(u, 4) for u in range(0, TU, 4)]
    spots = [(grid_in.at[cut], grid_ref.at[cut], grid_out.at[cut]) for cut in cuts]
    spots.append((cont_in, cont_ref, cont_out))
    takes = [pltpu.make_async_copy(src, via, in_sem.at[i]) for i, (src, via, dst) in enumerate(spots)]
    gives = [pltpu.make_async_copy(via, dst, out_sem.at[i]) for i, (src, via, dst) in enumerate(spots)]
    for take in takes:
        take.start()
    for take, give in zip(takes, gives):
        take.wait()
        give.start()
    for give in gives:
        give.wait()


def per_device(visibilities, owner_tile, cell_row, cell_col, subcell, channel_weight):
    anywhere = pl.BlockSpec(memory_space=pl.ANY)
    shapes = (jax.ShapeDtypeStruct((TU, TV, COLS), F32), jax.ShapeDtypeStruct((TU, TV), F32))
    grid, cont = pl.pallas_call(
        kernel,
        out_shape=shapes,
        in_specs=[anywhere] * 6,
        out_specs=(anywhere, anywhere),
        scratch_shapes=[
            pltpu.VMEM((ROWS, COLS), BF16),
            pltpu.VMEM((1, ROWS), I32),
            pltpu.VMEM((1, ROWS), I32),
            pltpu.VMEM((1, ROWS), I32),
            pltpu.VMEM((2, ROWS), I32),
            pltpu.VMEM((1, COLS // 2), F32),
            pltpu.VMEM((TU, TV, COLS), F32),
            pltpu.VMEM((TU, TV), F32),
            pltpu.VMEM((TU, 8, COLS), F32),
            pltpu.VMEM((8, EV, COLS), F32),
            pltpu.VMEM((TILES, CAP, COLS), BF16),
            pltpu.VMEM((STEPS, CAP, COLS), BF16),
            pltpu.VMEM((TILES, 1, 128), F32),
            pltpu.VMEM((STEPS, 1, 128), F32),
            pltpu.VMEM((1, ROWS), I32),
            pltpu.VMEM((EU, 2 * DEPTH), F32),
            pltpu.VMEM((EV, 2 * DEPTH), F32),
            pltpu.VMEM((2, 4 * TV, COLS), BF16),
            pltpu.VMEM((2, 4 * TV, COLS), BF16),
            pltpu.VMEM((TU * 8, COLS), BF16),
            pltpu.VMEM((2, TU * 8, COLS), BF16),
            pltpu.VMEM((64, COLS), BF16),
            pltpu.VMEM((4, 64, COLS), BF16),
            pltpu.VMEM((2, EU, TV), F32),
            pltpu.VMEM((2, EU, TV), F32),
            pltpu.VMEM((TU, TV), F32),
            pltpu.VMEM((2, 2, 8, TV), F32),
            pltpu.VMEM((2, 2, TU, TV), F32),
            pltpu.VMEM((2, 4, 8, TV), F32),
            pltpu.SemaphoreType.DMA((6,)),
            pltpu.SemaphoreType.DMA((5,)),
            pltpu.SemaphoreType.DMA((2,)),
            pltpu.SemaphoreType.DMA((2, GROUPS)),
            pltpu.SemaphoreType.DMA((8,)),
            pltpu.SemaphoreType.DMA((8,)),
            pltpu.SemaphoreType.DMA((17,)),
            pltpu.SemaphoreType.DMA((17,)),
            pltpu.SemaphoreType.REGULAR,
            pltpu.SemaphoreType.REGULAR,
        ],
        compiler_params=pltpu.CompilerParams(
            collective_id=0, has_side_effects=True, vmem_limit_bytes=62 * 2**20
        ),
        name="gridding",
    )(
        visibilities, owner_tile.reshape(1, ROWS), cell_row.reshape(1, ROWS),
        cell_col.reshape(1, ROWS), subcell, channel_weight.reshape(1, COLS // 2),
    )
    grid, cont = pl.pallas_call(
        handover,
        out_shape=shapes,
        in_specs=[anywhere] * 2,
        out_specs=(anywhere, anywhere),
        scratch_shapes=[
            pltpu.VMEM((TU, TV, COLS), F32),
            pltpu.VMEM((TU, TV), F32),
            pltpu.SemaphoreType.DMA((9,)),
            pltpu.SemaphoreType.DMA((9,)),
        ],
        compiler_params=pltpu.CompilerParams(vmem_limit_bytes=62 * 2**20),
        name="handover",
    )(grid, cont)
    return grid, cont.reshape(1, TU, TV)


def solution(mesh):
    in_specs = (
        P(("au", "vert"), "ch"),
        P(("au", "vert"), None),
        P(("au", "vert")),
        P(("au", "vert")),
        P(None, ("au", "vert")),
        P("ch"),
    )
    out_specs = (P("au", "vert", "ch"), P("ch", "au", "vert"))
    return jax.shard_map(
        per_device, mesh=mesh, in_specs=in_specs, out_specs=out_specs, check_vma=False
    )
```

time: 87.3 us -> 52.6 us (0.60)
  Pallas kernels: 80.4 us -> 51.9 us
  local copies, waits for them, and re-layouts: 5.21 us -> 0 us
    pallas_call x1 -> x2, Pallas kernels: 80.4 us -> 51.9 us  [the longest x1 49.5 us: per_device(): pl.pallas_call(kernel, out_shape=shapes, in_specs=[anywhere] * 6, out_spe...]
    unnamed x6 -> x0, local copies, waits for them, and re-layouts: 3.56 us -> none
where the time goes in v2:
time: 52.6 us; the launch traced here: 52.5 us
  Pallas kernels  51.9 us (99%)
  between operations  0.64 us (1%)
    pallas_call x1, Pallas kernels, per_device(): pl.pallas_call(kernel, out_shape=shapes, in_specs=[anywhere] * 6, out_spe...  49.5 us
    pallas_call x1, Pallas kernels, per_device(): pl.pallas_call(handover, out_shape=shapes, in_specs=[anywhere] * 2, out_s...  2.41 us

profile of v2, /device:TPU:1, one launch (start us, length us, event | category | flops | bytes accessed | tf_op | source)
XLA Modules:
  0.0 52.5 jit_solution(7791161972647907411)
XLA Ops:
  0.6 49.5 %gridding.1 = (f32[32,128,128]{2,1,0:T(8,128)}, f32[32,128]{1,0:T(8,128)}) custom-call(bf16[1024,128]{1,0:T(8,128)(2,1)} %vis_hbm.1, s32[1,1024]{1,0:T(1,128)} %bitcast.5, s32[1,1024]{1,0:T(1,128)} %bitcast.6, s32[1,1024]{1,0:T(1,128)} %bitcast.7, s32[2,1024]{1,0:T(2,128)} %sub_hbm.1, f32[1,64]{1,0:T(1,128)} %bitcast.8), custom_call_target="tpu_custom_call" | custom-call | tf_op jit(solution)/shard_map/gridding/pallas_call | solution.py:385
  50.1 2.4 %handover.1 = (f32[32,128,128]{2,1,0:T(8,128)}, f32[32,128]{1,0:T(8,128)}) custom-call(f32[32,128,128]{2,1,0:T(8,128)} %get-tuple-element.6.grid_in, f32[32,128]{1,0:T(8,128)} %get-tuple-element.7.cont_in), custom_call_target="tpu_custom_call" | custom-call | tf_op jit(solution)/shard_map/handover/pallas_call | solution.py:439

commit v3 on v2

--- a/solution.py
+++ b/solution.py
@@ -26,7 +26,6 @@
 GROUPS = STEPS // GROUP
 DEPTH = GROUP * CAP
 UB = 4
-EARLY = 4
 
 
 def mod(value, by):
@@ -51,15 +50,15 @@
     vis_ref, tile_ref, cell_row_ref, cell_col_ref, sub_ref, weight_ref, grid_ref, cont_ref,
     col_acc, row_acc, send_v, recv_v, send_m, recv_m, sid_ref, wr_ref, wc_ref,
     row_out, row_in, col_out, col_in, cor_out, cor_in,
-    sum_main, sum_edge, sum_mid_in, sum_row_in, sum_col_in, sum_cor_in,
-    load_sem, store_sem, send_sem, recv_sem, hsend_sem, hrecv_sem, ssend_sem, srecv_sem, line_sem, twin_sem,
+    sums, sum_row_in, sum_col_in, sum_cor_in, twin_out, twin_in,
+    load_sem, store_sem, send_sem, recv_sem, hsend_sem, hrecv_sem, ssend_sem, srecv_sem, twin_sem, stack_sem,
 ):
     au, vert, ch = lax.axis_index("au"), lax.axis_index("vert"), lax.axis_index("ch")
     z, xl = lax.rem(vert, 8), vert // 8
     y, core = au // 2, lax.rem(au, 2)
 
     def target(group, dz):
-        dc, dx, dy = lax.rem(group, 2), lax.rem(group // 2, 2), group // 4
+        dx, dc, dy = lax.rem(group, 2), lax.rem(group // 2, 2), group // 4
         to_au = mod(y + dy, 4) * 2 + mod(core + dc, 2)
         to_vert = mod(xl + dx, 2) * 8 + mod(z + dz, 8)
         return to_au, to_vert
@@ -78,25 +77,18 @@
     def greet(to_au, to_vert, to_ch, sem):
         pl.semaphore_signal(sem, inc=1, device_id=(to_au, to_vert, to_ch), device_id_type=MESH)
 
-    def greet_line(sem):
-        for dz in range(1, 8):
-            greet(*target(0, dz), ch, sem)
-
-    greet_line(barrier)
-    for group in range(1, GROUPS):
-        greet(*target(group, 0), ch, barrier)
+    def greet_stack(sem):
+        for group in range(2, GROUPS, 2):
+            greet(*target(group, 0), ch, sem)
+
+    for step in range(1, 2 * GROUP):
+        greet(*target(step // GROUP, step % GROUP), ch, barrier)
+    greet_stack(barrier)
     greet(au, vert, 1 - ch, barrier)
-    grid_ref[...] = jnp.zeros_like(grid_ref)
-    col_acc[...] = jnp.zeros_like(col_acc)
-    row_acc[...] = jnp.zeros_like(row_acc)
-    sum_edge[...] = jnp.zeros_like(sum_edge)
     for load in loads:
         load.wait()
 
     tile_row = tile_ref[...]
-    low = (sub_ref[0:1, :] * OVS + sub_ref[1:2, :]).astype(F32)
-    middle = cell_col_ref[...].astype(F32)
-    high = cell_row_ref[...].astype(F32)
     strict = flag(
         lax.broadcasted_iota(I32, (128, 128), 0) < lax.broadcasted_iota(I32, (128, 128), 1)
     ).astype(BF16)
@@ -104,9 +96,6 @@
     lane_iota = lax.broadcasted_iota(I32, (128, 128), 1)
     ones = jnp.ones((128, 128), BF16)
     before = jnp.zeros((TILES, 128), F32)
-    meta_low = jnp.zeros((TILES, 128), F32)
-    meta_middle = jnp.zeros((TILES, 128), F32)
-    meta_high = jnp.zeros((TILES, 128), F32)
     for part in range(ROWS // 128):
         cut = slice(part * 128, part * 128 + 128)
         hit = flag(sub_iota == tile_row[:, cut])
@@ -115,28 +104,42 @@
         before = before + nn(hit_low, ones)
         place = jnp.sum(hit * rank, axis=0, keepdims=True).astype(I32)
         sid_ref[:, cut] = tile_row[:, cut] * CAP + place
-        lane_hit = flag((sub_iota & (CAP - 1)) == place).astype(BF16)
-        meta_low += nt((hit * low[:, cut]).astype(BF16), lane_hit)
-        meta_middle += nt((hit * middle[:, cut]).astype(BF16), lane_hit)
-        meta_high += nt((hit * high[:, cut]).astype(BF16), lane_hit)
-    meta = meta_high * 8192.0 + meta_middle * 64.0 + meta_low
-    quarter = lane_iota // CAP
-    meta = jnp.where(quarter == lax.rem(sub_iota - z + 8, 4), meta, 0.0)
-    send_m[...] = meta.reshape(TILES, 1, 128)
-
-    def copies(group, dz):
+
+    spread = flag(
+        lax.broadcasted_iota(I32, (COLS // 2, COLS), 0) == lax.broadcasted_iota(I32, (COLS // 2, COLS), 1) // 2
+    ).astype(BF16)
+
+    def thirds(values):
+        pieces = []
+        for _ in range(3):
+            pieces.append(values.astype(BF16))
+            values = values - pieces[-1].astype(F32)
+        return pieces
+
+    weight = sum(nn(piece, spread) for piece in thirds(weight_ref[...]))
+    line = lax.broadcasted_iota(I32, (16, COLS), 0)
+    mine_only = (line & 1) == (lax.broadcasted_iota(I32, (16, COLS), 1) & 1)
+    pick = jnp.zeros((16, COLS), F32)
+    for i, piece in enumerate(thirds(weight)):
+        pick = jnp.where(mine_only & (line // 2 == i), piece.astype(F32), pick)
+    both = nt(pick.astype(BF16), vis_ref[...])
+    twin_out[...] = (both[0:2] + both[2:4] + both[4:6]).reshape(2, 1, ROWS)
+    swap = pltpu.make_async_remote_copy(
+        src_ref=twin_out.at[1 - ch], dst_ref=twin_in, send_sem=twin_sem.at[0], recv_sem=twin_sem.at[1],
+        device_id=(au, vert, 1 - ch), device_id_type=MESH,
+    )
+
+    def copy_of(kind, group, dz):
         to_au, to_vert = target(group, dz)
         tile = to_au * 16 + to_vert
         step = group * GROUP + dz
         device = (to_au, to_vert, ch)
-        return [
-            pltpu.make_async_remote_copy(
-                src_ref=src.at[tile], dst_ref=dst.at[step],
-                send_sem=send_sem.at[kind], recv_sem=recv_sem.at[kind, group],
-                device_id=device, device_id_type=MESH,
-            )
-            for kind, (src, dst) in enumerate([(send_v, recv_v), (send_m, recv_m)])
-        ]
+        src, dst = [(send_v, recv_v), (send_m, recv_m)][kind]
+        return pltpu.make_async_remote_copy(
+            src_ref=src.at[tile], dst_ref=dst.at[step],
+            send_sem=send_sem.at[kind], recv_sem=recv_sem.at[kind, group],
+            device_id=device, device_id_type=MESH,
+        )
 
     def fill(group):
         to_au, to_vert = target(group, 0)
@@ -145,30 +148,58 @@
         pick = flag(slot == sid_ref[...]).astype(BF16)
         send_v[pl.ds(base, GROUP)] = nn(pick, vis_ref[...]).astype(BF16).reshape(GROUP, CAP, COLS)
 
-    def start(group, first):
+    def start(kind, group, first):
         for dz in range(first, GROUP):
-            for copy in copies(group, dz):
-                copy.start()
-
+            copy_of(kind, group, dz).start()
+
+    fill(0)
     pl.semaphore_wait(barrier, 23)
-    greet_line(line_sem)
-    fill(0)
-    start(0, 1)
+    greet_stack(stack_sem)
+    start(0, 0, 1)
+    swap.start()
+    fill(1)
+    start(0, 1, 0)
     mine = au * 16 + vert
     recv_v[0] = send_v[mine]
+    fill(2)
+    fill(3)
+    pl.semaphore_wait(stack_sem, 7)
+    start(0, 2, 0)
+    start(0, 3, 0)
+
+    low = (sub_ref[0:1, :] * OVS + sub_ref[1:2, :]).astype(F32)
+    middle = cell_col_ref[...].astype(F32)
+    high = cell_row_ref[...].astype(F32)
+    swap.wait()
+    fields = [high, middle, low]
+    fields += [piece.astype(F32) for piece in thirds(twin_out[ch] + twin_in[...])]
+    slots = jnp.zeros((len(fields) * TILES, 128), F32)
+    for part in range(ROWS // 128):
+        cut = slice(part * 128, part * 128 + 128)
+        hit = flag(sub_iota == tile_row[:, cut])
+        lane_hit = flag((sub_iota & (CAP - 1)) == (sid_ref[:, cut] & (CAP - 1))).astype(BF16)
+        slots += nt(jnp.concatenate([hit * field[:, cut] for field in fields], axis=0).astype(BF16), lane_hit)
+    slots = [slots[i * TILES : i * TILES + TILES] for i in range(len(fields))]
+    meta = slots[0] * 8192.0 + slots[1] * 64.0 + slots[2]
+    quarter = lane_iota // CAP
+    turn = lax.rem(sub_iota - z + 8, 4)
+    meta = jnp.where(quarter == turn, meta, 0.0)
+    meta = jnp.where(quarter == ((turn + 1) & 3), slots[3] + slots[4] + slots[5], meta)
+    send_m[...] = meta.reshape(TILES, 1, 128)
     recv_m[0] = send_m[mine]
-    for group in range(1, EARLY):
-        fill(group)
-    pl.semaphore_wait(line_sem, 7)
-    greet(au, vert, 1 - ch, twin_sem)
-    for group in range(1, EARLY):
-        start(group, 0)
+    for group in range(4):
+        start(1, group, 1 if group == 0 else 0)
+    grid_ref[...] = jnp.zeros_like(grid_ref)
+    col_acc[...] = jnp.zeros_like(col_acc)
+    row_acc[...] = jnp.zeros_like(row_acc)
+    sums[...] = jnp.zeros_like(sums)
 
     def fill_step(group, carry):
         fill(group)
-        start(group, 0)
+        start(0, group, 0)
+        start(1, group, 0)
         return carry
-    lax.fori_loop(EARLY, GROUPS, fill_step, 0)
+    lax.fori_loop(4, GROUPS, fill_step, 0)
 
     def weights(meta_line):
         m = meta_line.astype(I32)
@@ -189,17 +220,21 @@
         for kind, ref in enumerate([recv_v, recv_m]):
             pltpu.make_async_copy(ref.at[span], ref.at[span], recv_sem.at[kind, group]).wait()
 
-    def add_chunk(group, groups, after_rows):
+    def add_chunk(group, groups, before_rows, after_rows):
         base = group * GROUP
         depth = groups * DEPTH
-        line = jnp.concatenate(
-            [
-                jnp.sum(recv_m[pl.ds(base + 4 * i, 4)].reshape(4, 128), axis=0, keepdims=True)
-                for i in range(2 * groups)
-            ],
-            axis=1,
-        )
-        weights(line)
+        quarter = lax.broadcasted_iota(I32, (4, 128), 1) // CAP == lax.broadcasted_iota(I32, (4, 128), 0)
+        metas, totals = [], []
+        for i in range(2 * groups):
+            lines = recv_m[pl.ds(base + 4 * i, 4)].reshape(4, 128)
+            metas.append(jnp.sum(jnp.where(quarter, lines, 0.0), axis=0, keepdims=True))
+            lines = pltpu.roll(lines, 128 - CAP, 1)
+            totals.append(jnp.sum(jnp.where(quarter, lines, 0.0), axis=0, keepdims=True))
+        weights(jnp.concatenate(metas, axis=1))
+        left_high, left_low, _ = thirds(wr_ref[:, 0:depth] * jnp.concatenate(totals, axis=1))
+        right_high, right_low, _ = thirds(wc_ref[:, 0:depth])
+        sums[:, 0:EV] += nt(left_high, right_high) + nt(left_low, right_high) + nt(left_high, right_low)
+        before_rows()
         values = recv_v[pl.ds(base, groups * GROUP)].reshape(depth, COLS)
         for u in [*range(TU, EU, UB), *range(0, TU, UB)]:
             if u == 0:
@@ -214,13 +249,13 @@
                 row_acc[u - TU : u - TU + UB] += product
 
     arrived(0, 1, GROUP - 1)
-    add_chunk(0, 1, lambda: None)
+    add_chunk(0, 1, lambda: None, lambda: None)
 
     def chunk_step(pair, carry):
         group = 2 * pair + 1
         arrived(group, 0, GROUP)
         arrived(group + 1, 0, GROUP)
-        add_chunk(group, 2, lambda: None)
+        add_chunk(group, 2, lambda: None, lambda: None)
         return carry
     lax.fori_loop(0, GROUPS // 2 - 1, chunk_step, 0)
     down, up = mod(au + 1, 8), mod(au + 7, 8)
@@ -251,67 +286,34 @@
         for copy in row_halos:
             copy.start()
 
+    def part(src, dst, number, to_au, to_vert):
+        return pltpu.make_async_remote_copy(
+            src_ref=src, dst_ref=dst, send_sem=ssend_sem.at[number], recv_sem=srecv_sem.at[number],
+            device_id=(to_au, to_vert, ch), device_id_type=MESH,
+        )
+
+    row_sums = sums.at[pl.ds(TU, 8), pl.ds(0, TV)]
+    col_sums = sums.at[pl.ds(0, TU), pl.ds(TV, TV)]
+    cor_sums = sums.at[pl.ds(TU, 8), pl.ds(TV, TV)]
+    parts = [
+        part(row_sums, sum_row_in.at[0], 0, down, vert),
+        part(row_sums, sum_row_in.at[1], 1, up, vert),
+        part(col_sums, sum_col_in.at[0], 2, au, right),
+        part(col_sums, sum_col_in.at[1], 3, au, left),
+        part(cor_sums, sum_cor_in.at[0], 4, down, right),
+        part(cor_sums, sum_cor_in.at[1], 5, down, left),
+        part(cor_sums, sum_cor_in.at[2], 6, up, right),
+        part(cor_sums, sum_cor_in.at[3], 7, up, left),
+    ]
+
+    def send_sums():
+        for copy in parts:
+            copy.start()
+
     arrived(GROUPS - 1, 0, GROUP)
-    add_chunk(GROUPS - 1, 1, send_rows)
+    add_chunk(GROUPS - 1, 1, send_sums, send_rows)
     col_out[...] = col_acc[...].reshape(TU * 8, COLS).astype(BF16)
     for copy in col_halos:
-        copy.start()
-
-    spread = flag(
-        lax.broadcasted_iota(I32, (COLS // 2, COLS), 0) == lax.broadcasted_iota(I32, (COLS // 2, COLS), 1) // 2
-    ).astype(BF16)
-    weight = jnp.zeros((1, COLS), F32)
-    rest = weight_ref[...]
-    for part in range(3):
-        piece = rest.astype(BF16)
-        rest = rest - piece.astype(F32)
-        weight += nn(piece, spread)
-    weight_high = weight.astype(BF16).astype(F32)
-    line = lax.broadcasted_iota(I32, (16, COLS), 0)
-    mine_only = (line & 1) == (lax.broadcasted_iota(I32, (16, COLS), 1) & 1)
-    pick = jnp.where(line < 2, weight_high, jnp.where(line < 4, weight - weight_high, 0.0))
-    pick = jnp.where(mine_only, pick, 0.0).astype(BF16)
-    pick = jnp.concatenate([pick, pick], axis=1)
-
-    def channel_sum(u):
-        if u < TU:
-            cells = jnp.concatenate([grid_ref[u], col_acc[u]], axis=0)
-        else:
-            cells = row_acc[u - TU]
-        cells_high = cells.astype(BF16)
-        cells_low = (cells - cells_high.astype(F32)).astype(BF16)
-        result = nt(pick, jnp.concatenate([cells_high, cells_low], axis=1))
-        return result[0:2] + result[2:4]
-
-    for u in range(0, EU, 8):
-        sums = [channel_sum(u + i) for i in range(8)]
-        for q in range(2):
-            whole = jnp.concatenate([one[q : q + 1] for one in sums], axis=0)
-            sum_main[q, u : u + 8, :] = whole[:, 0:TV]
-            sum_edge[q, u : u + 8, 0:8] = whole[:, TV:EV]
-
-    def part(src, dst, number, to_au, to_vert, to_ch):
-        return pltpu.make_async_remote_copy(
-            src_ref=src, dst_ref=dst, send_sem=ssend_sem.at[number], recv_sem=srecv_sem.at[number],
-            device_id=(to_au, to_vert, to_ch), device_id_type=MESH,
-        )
-
-    parts = [part(sum_main.at[1 - ch, pl.ds(0, TU)], sum_mid_in, 0, au, vert, 1 - ch)]
-    for other in range(2):
-        q = 1 - ch if other else ch
-        rows, cols, edge = pl.ds(TU, 8), pl.ds(0, TU), 1 + 8 * other
-        parts += [
-            part(sum_main.at[q, rows], sum_row_in.at[other, 0], edge, down, vert, q),
-            part(sum_main.at[q, rows], sum_row_in.at[other, 1], edge + 1, up, vert, q),
-            part(sum_edge.at[q, cols], sum_col_in.at[other, 0], edge + 2, au, right, q),
-            part(sum_edge.at[q, cols], sum_col_in.at[other, 1], edge + 3, au, left, q),
-            part(sum_edge.at[q, rows], sum_cor_in.at[other, 0], edge + 4, down, right, q),
-            part(sum_edge.at[q, rows], sum_cor_in.at[other, 1], edge + 5, down, left, q),
-            part(sum_edge.at[q, rows], sum_cor_in.at[other, 2], edge + 6, up, right, q),
-            part(sum_edge.at[q, rows], sum_cor_in.at[other, 3], edge + 7, up, left, q),
-        ]
-    pl.semaphore_wait(twin_sem, 1)
-    for copy in parts:
         copy.start()
 
     for kind, ref in enumerate([recv_v, recv_m]):
@@ -348,13 +350,9 @@
         at = lane[0:rows]
         return jnp.where(at < 4, from_left, 0.0) + jnp.where(at >= TV - 4, pltpu.roll(from_right, TV - 8, 1), 0.0)
 
-    total = sum_main[ch, 0:TU] + sum_mid_in[...]
-    first = jnp.zeros((8, TV), F32)
-    last = jnp.zeros((8, TV), F32)
-    for other in range(2):
-        total += sides(sum_col_in[other, 0], sum_col_in[other, 1], TU)
-        first += sum_row_in[other, 0] + sides(sum_cor_in[other, 0], sum_cor_in[other, 1], 8)
-        last += sum_row_in[other, 1] + sides(sum_cor_in[other, 2], sum_cor_in[other, 3], 8)
+    total = sums[0:TU, 0:TV] + sides(sum_col_in[0], sum_col_in[1], TU)
+    first = sum_row_in[0] + sides(sum_cor_in[0], sum_cor_in[1], 8)
+    last = sum_row_in[1] + sides(sum_cor_in[2], sum_cor_in[3], 8)
     cont_ref[...] = total * (1.0 / CHAN)
     cont_ref[0:8] += jnp.where(top, first, 0.0) * (1.0 / CHAN)
     cont_ref[TU - 8 : TU] += jnp.where(top, 0.0, last) * (1.0 / CHAN)
@@ -411,21 +409,21 @@
             pltpu.VMEM((2, TU * 8, COLS), BF16),
             pltpu.VMEM((64, COLS), BF16),
             pltpu.VMEM((4, 64, COLS), BF16),
-            pltpu.VMEM((2, EU, TV), F32),
-            pltpu.VMEM((2, EU, TV), F32),
-            pltpu.VMEM((TU, TV), F32),
-            pltpu.VMEM((2, 2, 8, TV), F32),
-            pltpu.VMEM((2, 2, TU, TV), F32),
-            pltpu.VMEM((2, 4, 8, TV), F32),
+            pltpu.VMEM((EU, 2 * TV), F32),
+            pltpu.VMEM((2, 8, TV), F32),
+            pltpu.VMEM((2, TU, TV), F32),
+            pltpu.VMEM((4, 8, TV), F32),
+            pltpu.VMEM((2, 1, ROWS), F32),
+            pltpu.VMEM((1, ROWS), F32),
             pltpu.SemaphoreType.DMA((6,)),
             pltpu.SemaphoreType.DMA((5,)),
             pltpu.SemaphoreType.DMA((2,)),
             pltpu.SemaphoreType.DMA((2, GROUPS)),
             pltpu.SemaphoreType.DMA((8,)),
             pltpu.SemaphoreType.DMA((8,)),
-            pltpu.SemaphoreType.DMA((17,)),
-            pltpu.SemaphoreType.DMA((17,)),
-            pltpu.SemaphoreType.REGULAR,
+            pltpu.SemaphoreType.DMA((8,)),
+            pltpu.SemaphoreType.DMA((8,)),
+            pltpu.SemaphoreType.DMA((2,)),
             pltpu.SemaphoreType.REGULAR,
         ],
         compiler_params=pltpu.CompilerParams(

time: 52.6 us -> 49.6 us (0.943)
  Pallas kernels: 51.9 us -> 48.8 us
    pallas_call x1, Pallas kernels: 49.5 us -> 46.4 us  [per_device(): pl.pallas_call(kernel, out_shape=shapes, in_specs=[anywhere] * 6, out_spe...]
where the time goes in v3:
time: 49.6 us; the launch traced here: 49.4 us
  Pallas kernels  48.8 us (98%)
  between operations  0.64 us (1%)
    pallas_call x1, Pallas kernels, per_device(): pl.pallas_call(kernel, out_shape=shapes, in_specs=[anywhere] * 6, out_spe...  46.4 us
    pallas_call x1, Pallas kernels, per_device(): pl.pallas_call(handover, out_shape=shapes, in_specs=[anywhere] * 2, out_s...  2.41 us

profile of v3, /device:TPU:1, one launch (start us, length us, event | category | flops | bytes accessed | tf_op | source)
XLA Modules:
  0.0 49.4 jit_solution(17537471987904308435)
XLA Ops:
  0.6 46.4 %gridding.1 = (f32[32,128,128]{2,1,0:T(8,128)}, f32[32,128]{1,0:T(8,128)}) custom-call(bf16[1024,128]{1,0:T(8,128)(2,1)} %vis_hbm.1, s32[1,1024]{1,0:T(1,128)} %bitcast.5, s32[1,1024]{1,0:T(1,128)} %bitcast.6, s32[1,1024]{1,0:T(1,128)} %bitcast.7, s32[2,1024]{1,0:T(2,128)} %sub_hbm.1, f32[1,64]{1,0:T(1,128)} %bitcast.8), custom_call_target="tpu_custom_call" | custom-call | tf_op jit(solution)/shard_map/gridding/pallas_call | solution.py:383
  47.0 2.4 %handover.1 = (f32[32,128,128]{2,1,0:T(8,128)}, f32[32,128]{1,0:T(8,128)}) custom-call(f32[32,128,128]{2,1,0:T(8,128)} %get-tuple-element.6.grid_in, f32[32,128]{1,0:T(8,128)} %get-tuple-element.7.cont_in), custom_call_target="tpu_custom_call" | custom-call | tf_op jit(solution)/shard_map/handover/pallas_call | solution.py:437

commit v4 on v3

--- a/solution.py
+++ b/solution.py
@@ -316,6 +316,20 @@
     for copy in col_halos:
         copy.start()
 
+    inner_rows = pl.ds(4, TU - 8)
+    blocks = [
+        (inner_rows, pl.ds(8, TV - 16)),
+        (pl.ds(0, 4), pl.ds(0, TV)),
+        (pl.ds(TU - 4, 4), pl.ds(0, TV)),
+        (inner_rows, pl.ds(0, 8)),
+        (inner_rows, pl.ds(TV - 8, 8)),
+    ]
+    stores = [
+        pltpu.make_async_copy(grid_ref.at[block], grid_hbm.at[block], store_sem.at[i])
+        for i, block in enumerate(blocks)
+    ]
+    stores[0].start()
+
     for kind, ref in enumerate([recv_v, recv_m]):
         span = pl.ds(1, STEPS - 1)
         pltpu.make_async_copy(ref.at[span], ref.at[span], send_sem.at[kind]).wait()
@@ -335,11 +349,7 @@
     grid_ref[TU - 4 : TU, 0:8] += jnp.where(front, corners[2][4:8], 0.0)
     grid_ref[TU - 4 : TU, TV - 8 : TV] += jnp.where(front, 0.0, corners[3][4:8])
 
-    stores = [
-        pltpu.make_async_copy(grid_ref.at[pl.ds(u, 8)], grid_hbm.at[pl.ds(u, 8)], store_sem.at[u // 8])
-        for u in range(0, TU, 8)
-    ]
-    for store in stores:
+    for store in stores[1:]:
         store.start()
     for copy in parts:
         copy.wait()
@@ -356,7 +366,7 @@
     cont_ref[...] = total * (1.0 / CHAN)
     cont_ref[0:8] += jnp.where(top, first, 0.0) * (1.0 / CHAN)
     cont_ref[TU - 8 : TU] += jnp.where(top, 0.0, last) * (1.0 / CHAN)
-    store = pltpu.make_async_copy(cont_ref, cont_hbm, store_sem.at[4])
+    store = pltpu.make_async_copy(cont_ref, cont_hbm, store_sem.at[5])
     store.start()
     for store in [*stores, store]:
         store.wait()
@@ -416,7 +426,7 @@
             pltpu.VMEM((2, 1, ROWS), F32),
             pltpu.VMEM((1, ROWS), F32),
             pltpu.SemaphoreType.DMA((6,)),
-            pltpu.SemaphoreType.DMA((5,)),
+            pltpu.SemaphoreType.DMA((6,)),
             pltpu.SemaphoreType.DMA((2,)),
             pltpu.SemaphoreType.DMA((2, GROUPS)),
             pltpu.SemaphoreType.DMA((8,)),

time: 49.6 us -> 49.1 us (0.990)
  no operation moved by 1% of the time
where the time goes in v4:
time: 49.1 us; the launch traced here: 49 us
  Pallas kernels  48.4 us (99%)
  between operations  0.64 us (1%)
    pallas_call x1, Pallas kernels, per_device(): pl.pallas_call(kernel, out_shape=shapes, in_specs=[anywhere] * 6, out_spe...  45.9 us
    pallas_call x1, Pallas kernels, per_device(): pl.pallas_call(handover, out_shape=shapes, in_specs=[anywhere] * 2, out_s...  2.41 us

profile of v4, /device:TPU:1, one launch (start us, length us, event | category | flops | bytes accessed | tf_op | source)
XLA Modules:
  0.0 49.0 jit_solution(4335572683404589610)
XLA Ops:
  0.6 45.9 %gridding.1 = (f32[32,128,128]{2,1,0:T(8,128)}, f32[32,128]{1,0:T(8,128)}) custom-call(bf16[1024,128]{1,0:T(8,128)(2,1)} %vis_hbm.1, s32[1,1024]{1,0:T(1,128)} %bitcast.5, s32[1,1024]{1,0:T(1,128)} %bitcast.6, s32[1,1024]{1,0:T(1,128)} %bitcast.7, s32[2,1024]{1,0:T(2,128)} %sub_hbm.1, f32[1,64]{1,0:T(1,128)} %bitcast.8), custom_call_target="tpu_custom_call" | custom-call | tf_op jit(solution)/shard_map/gridding/pallas_call | solution.py:393
  46.6 2.4 %handover.1 = (f32[32,128,128]{2,1,0:T(8,128)}, f32[32,128]{1,0:T(8,128)}) custom-call(f32[32,128,128]{2,1,0:T(8,128)} %get-tuple-element.6.grid_in, f32[32,128]{1,0:T(8,128)} %get-tuple-element.7.cont_in), custom_call_target="tpu_custom_call" | custom-call | tf_op jit(solution)/shard_map/handover/pallas_call | solution.py:447

commit v5 on v4

--- a/solution.py
+++ b/solution.py
@@ -333,6 +333,23 @@
     for kind, ref in enumerate([recv_v, recv_m]):
         span = pl.ds(1, STEPS - 1)
         pltpu.make_async_copy(ref.at[span], ref.at[span], send_sem.at[kind]).wait()
+    for copy in parts:
+        copy.wait()
+    top = lax.broadcasted_iota(I32, (8, TV), 0) < 4
+    lane = lax.broadcasted_iota(I32, (TU, TV), 1)
+
+    def sides(from_left, from_right, rows):
+        at = lane[0:rows]
+        return jnp.where(at < 4, from_left, 0.0) + jnp.where(at >= TV - 4, pltpu.roll(from_right, TV - 8, 1), 0.0)
+
+    total = sums[0:TU, 0:TV] + sides(sum_col_in[0], sum_col_in[1], TU)
+    first = sum_row_in[0] + sides(sum_cor_in[0], sum_cor_in[1], 8)
+    last = sum_row_in[1] + sides(sum_cor_in[2], sum_cor_in[3], 8)
+    cont_ref[...] = total * (1.0 / CHAN)
+    cont_ref[0:8] += jnp.where(top, first, 0.0) * (1.0 / CHAN)
+    cont_ref[TU - 8 : TU] += jnp.where(top, 0.0, last) * (1.0 / CHAN)
+    cont_store = pltpu.make_async_copy(cont_ref, cont_hbm, store_sem.at[5])
+    cont_store.start()
     for copy in row_halos + col_halos:
         copy.wait()
 
@@ -351,24 +368,7 @@
 
     for store in stores[1:]:
         store.start()
-    for copy in parts:
-        copy.wait()
-    top = lax.broadcasted_iota(I32, (8, TV), 0) < 4
-    lane = lax.broadcasted_iota(I32, (TU, TV), 1)
-
-    def sides(from_left, from_right, rows):
-        at = lane[0:rows]
-        return jnp.where(at < 4, from_left, 0.0) + jnp.where(at >= TV - 4, pltpu.roll(from_right, TV - 8, 1), 0.0)
-
-    total = sums[0:TU, 0:TV] + sides(sum_col_in[0], sum_col_in[1], TU)
-    first = sum_row_in[0] + sides(sum_cor_in[0], sum_cor_in[1], 8)
-    last = sum_row_in[1] + sides(sum_cor_in[2], sum_cor_in[3], 8)
-    cont_ref[...] = total * (1.0 / CHAN)
-    cont_ref[0:8] += jnp.where(top, first, 0.0) * (1.0 / CHAN)
-    cont_ref[TU - 8 : TU] += jnp.where(top, 0.0, last) * (1.0 / CHAN)
-    store = pltpu.make_async_copy(cont_ref, cont_hbm, store_sem.at[5])
-    store.start()
-    for store in [*stores, store]:
+    for store in [*stores, cont_store]:
         store.wait()
 
 

time: 49.1 us -> 49.1 us (level)
  no operation moved by 1% of the time
where the time goes in v5:
time: 49.1 us; the launch traced here: 49 us
  Pallas kernels  48.4 us (99%)
  between operations  0.64 us (1%)
    pallas_call x1, Pallas kernels, per_device(): pl.pallas_call(kernel, out_shape=shapes, in_specs=[anywhere] * 6, out_spe...  45.9 us
    pallas_call x1, Pallas kernels, per_device(): pl.pallas_call(handover, out_shape=shapes, in_specs=[anywhere] * 2, out_s...  2.41 us

profile of v5, /device:TPU:1, one launch (start us, length us, event | category | flops | bytes accessed | tf_op | source)
XLA Modules:
  0.0 49.0 jit_solution(13683477091879135268)
XLA Ops:
  0.6 45.9 %gridding.1 = (f32[32,128,128]{2,1,0:T(8,128)}, f32[32,128]{1,0:T(8,128)}) custom-call(bf16[1024,128]{1,0:T(8,128)(2,1)} %vis_hbm.1, s32[1,1024]{1,0:T(1,128)} %bitcast.5, s32[1,1024]{1,0:T(1,128)} %bitcast.6, s32[1,1024]{1,0:T(1,128)} %bitcast.7, s32[2,1024]{1,0:T(2,128)} %sub_hbm.1, f32[1,64]{1,0:T(1,128)} %bitcast.8), custom_call_target="tpu_custom_call" | custom-call | tf_op jit(solution)/shard_map/gridding/pallas_call | solution.py:393
  46.6 2.4 %handover.1 = (f32[32,128,128]{2,1,0:T(8,128)}, f32[32,128]{1,0:T(8,128)}) custom-call(f32[32,128,128]{2,1,0:T(8,128)} %get-tuple-element.6.grid_in, f32[32,128]{1,0:T(8,128)} %get-tuple-element.7.cont_in), custom_call_target="tpu_custom_call" | custom-call | tf_op jit(solution)/shard_map/handover/pallas_call | solution.py:447
